TPU v7x, 32 devices: a whole 2x2x4 slice. The times are simulated.
32 devices in a mesh: seq: 16 (over z, x, core), head: 2 (over y).
Axes of the slice: x: 2, y: 2, z: 4, core: 2. Of those that a mesh axis runs over, the one named last changes fastest.
Arguments:
- queries: bfloat16 [2048, 8, 1024], P(('seq', 'head')), may hold values from -256 to 256
- branch_key_value: bfloat16 [2048, 8, 256], P(('seq', 'head')), may hold values from -4 to 4
- branch_ids: int32 [2048], replicated, may hold values from 0 to 3, never falling along the last dimension, each value on 1 to 1024 neighbouring positions
- pool: bfloat16 [16, 16, 8, 256], P('seq', None, 'head'), may hold values from -4 to 4
- page_table: int32 [8, 8], P('head'), may hold values from 0 to 15, as said below
Outputs:
- attended: bfloat16 [2048, 8, 1024], P(('seq', 'head'))
Inputs may be any that keep to these rules, and one draw needn't show every extreme that they name: `branch_ids`: never falls along the rows; each branch covers 1 to 1024 rows and one covers exactly 1024. `page_table`: row h holds 8 distinct page numbers.
All inputs are finite; a program needn't handle non-finite values.
Results may differ from a plain program's by a relative error of at most 0.0085.
Values may be sent and summed in bfloat16 or wider, within the bound.
A program may use at most 64 MiB of HBM per device.

v0:
```python
import jax
import jax.numpy as jnp
from jax import lax
from jax.sharding import PartitionSpec as P

HEAD_DIM = 128


def passed_along(value, axis, by):
    count = lax.axis_size(axis)
    pairs = [(i, i + by) for i in range(count) if 0 <= i + by < count]
    return lax.ppermute(value, axis, pairs)


def blend_keys(state, query, pairs, allowed, scale):
    top, total, summed = state
    width = query.shape[-1]
    keys = pairs[..., :width]
    value_rows = pairs[..., width:]
    scores = jnp.einsum("rhgd,khd->rhgk", query, keys, preferred_element_type=jnp.float32) * scale
    scores = jnp.where(allowed, scores, -jnp.inf)
    new_top = jnp.maximum(top, jnp.max(scores, axis=-1))
    factor = jnp.exp(top - new_top)
    weights = jnp.exp(scores - new_top[..., None])
    total = total * factor + jnp.sum(weights, axis=-1)
    rounded = weights.astype(jnp.bfloat16)
    summed = summed * factor[..., None] + jnp.einsum(
        "rhgk,khd->rhgd", rounded, value_rows, preferred_element_type=jnp.float32
    )
    return (new_top, total, summed)


def per_device(queries, branch_key_value, branch_ids, pool, page_table):
    reach_count = min(32, lax.axis_size("seq") // 2)
    query, pairs = (
        lax.all_to_all(queries, "head", split_axis=1, concat_axis=0, tiled=True),
        lax.all_to_all(branch_key_value, "head", split_axis=1, concat_axis=0, tiled=True),
    )
    rows = query.shape[0]
    local_heads = query.shape[1]
    group = query.shape[2] // HEAD_DIM
    query = query.reshape(rows, local_heads, group, HEAD_DIM)
    scale = HEAD_DIM ** (-0.5)
    row_start = lax.axis_index("seq") * rows
    row_ids = jnp.arange(rows, dtype=jnp.int32)
    own_ids = lax.dynamic_slice_in_dim(branch_ids, row_start, rows, 0)
    own_rows = row_start + row_ids
    state = (
        jnp.full((rows, local_heads, group), -1e30, jnp.float32),
        jnp.zeros((rows, local_heads, group), jnp.float32),
        jnp.zeros((rows, local_heads, group, HEAD_DIM), jnp.float32),
    )
    page_rows = pool.shape[1]
    pair_width = pool.shape[3]
    piece = lax.all_gather(pool, "seq", axis=0, tiled=True)
    count = piece.shape[0]
    page_ids = jnp.arange(count, dtype=jnp.int32)
    chosen = jnp.any(page_table[:, :, None] == page_ids[None, None, :], axis=1)
    allowed = jnp.broadcast_to(chosen[:, :, None], (local_heads, count, page_rows))
    allowed = allowed.reshape(local_heads, count * page_rows)
    flat = piece.reshape(count * page_rows, local_heads, pair_width)

    def fold_in_piece(inner):
        return blend_keys(inner, query, flat, allowed[None, :, None, :], scale)

    def keep_state(inner):
        return inner

    state = lax.cond(jnp.any(chosen), fold_in_piece, keep_state, state)

    def causal_step(carry, block, back):
        key_start = row_start - back * rows
        key_ids = lax.dynamic_slice_in_dim(branch_ids, jnp.maximum(key_start, 0), rows, 0)
        key_rows = key_start + row_ids
        allowed = (
            (key_ids[None, :] == own_ids[:, None])
            & (key_rows[None, :] <= own_rows[:, None])
            & (key_start >= 0)
        )
        return blend_keys(carry, query, block, allowed[:, None, None, :], scale)

    state = causal_step(state, pairs, 0)
    for back in range(1, reach_count + 1):
        earlier = passed_along(pairs, "seq", back)
        state = causal_step(state, earlier, back)
    top, total, summed = state
    mixed = (
        (summed / total[..., None])
        .astype(jnp.bfloat16)
        .reshape(rows, local_heads, group * HEAD_DIM)
    )
    return lax.all_to_all(mixed, "head", split_axis=0, concat_axis=1, tiled=True)


def solution(mesh):
    return jax.shard_map(
        per_device,
        mesh=mesh,
        in_specs=(
            P(("seq", "head"), None, None),
            P(("seq", "head"), None, None),
            P(),
            P("seq", None, "head", None),
            P("head", None),
        ),
        out_specs=P(("seq", "head"), None, None),
        check_vma=False,
    )
```

profile of v0, /device:TPU:17, one launch (start us, length us, event | category | flops | bytes accessed | tf_op | source)
XLA Modules:
  0.0 151.9 jit_solution(2351721324200655206)
XLA Ops:
  0.0 1.7 %copy.104 = bf16[64,8,256]{2,0,1:T(8,128)(2,1)} copy(bf16[64,8,256]{2,1,0:T(8,128)(2,1)} %param.8) | data formatting | bytes 524288 | tf_op args[1]
  1.7 3.4 %all-to-all-start.1 = ((bf16[64,8,256]{2,0,1:T(8,128)(2,1)}), bf16[64,8,256]{2,0,1:T(8,128)(2,1)S(1)}, u32[]{:S(2)}, u32[]{:S(2)}) async-start(bf16[64,8,256]{2,0,1:T(8,128)(2,1)} %copy.104), calls=%async_computation.1 | async-start | bytes 524288 | tf_op jit(solution)/shard_map/all_to_all | solution.py:37
  5.2 1.2 fusion.81
  6.4 0.2 and_and_fusion.7
  6.6 1.5 iota_compare_fusion
  8.0 2.8 %copy.101 = bf16[64,8,1024]{2,0,1:T(8,128)(2,1)} copy(bf16[64,8,1024]{2,1,0:T(8,128)(2,1)} %param.7) | data formatting | bytes 2097152 | tf_op args[0]
  10.8 3.6 %all-to-all-start = ((bf16[64,8,1024]{2,0,1:T(8,128)(2,1)}), bf16[64,8,1024]{2,0,1:T(8,128)(2,1)S(1)}, u32[]{:S(2)}, u32[]{:S(2)}) async-start(bf16[64,8,1024]{2,0,1:T(8,128)(2,1)} %copy.101), calls=%async_computation | async-start | bytes 2097152 | tf_op jit(solution)/shard_map/all_to_all | solution.py:36
  15.1 0.9 and_and_fusion.8
  15.9 19.7 %all_gather.3 = bf16[16,16,4,256]{3,1,0,2:T(8,128)(2,1)} all-gather(bf16[1,16,4,256]{3,1,0,2:T(8,128)(2,1)S(1)} %copy.100), channel_id=1, replica_groups=mesh['seq'=16,'head'=2] {'seq'}, dimensions={0}, use_global_device_ids=true | all-gather | bytes 557056 | tf_op jit(solution)/shard_map/all_gather | solution.py:55
  35.6 1.3 collective-permute-start.7
  36.9 1.3 collective-permute-start.6
  38.2 4.0 %collective-permute-start.5 = (bf16[128,4,256]{2,0,1:T(8,128)(2,1)S(1)}, bf16[128,4,256]{2,0,1:T(8,128)(2,1)}, u32[]{:S(2)}, u32[]{:S(2)}) collective-permute-start(bf16[128,4,256]{2,0,1:T(8,128)(2,1)S(1)} %bitcast.242), channel_id=1, source_target_pairs={{0,12},{2,14},{4,16},{6,18},{8,20},{10,22},{12,24},{14,26},{16,28}... | collective-permute-start | bytes 786440 | tf_op jit(solution)/shard_map/ppermute | solution.py:12
  42.2 1.9 %collective-permute-start.4 = (bf16[128,4,256]{2,0,1:T(8,128)(2,1)S(1)}, bf16[128,4,256]{2,0,1:T(8,128)(2,1)}, u32[]{:S(2)}, u32[]{:S(2)}) collective-permute-start(bf16[128,4,256]{2,0,1:T(8,128)(2,1)S(1)} %bitcast.243), channel_id=1, source_target_pairs={{0,10},{2,12},{4,14},{6,16},{8,18},{10,20},{12,22},{14,24},{16,26}... | collective-permute-start | bytes 786440 | tf_op jit(solution)/shard_map/ppermute | solution.py:12
  44.1 1.9 %collective-permute-start = (bf16[128,4,256]{2,0,1:T(8,128)(2,1)S(1)}, bf16[128,4,256]{2,0,1:T(8,128)(2,1)}, u32[]{:S(2)}, u32[]{:S(2)}) collective-permute-start(bf16[128,4,256]{2,0,1:T(8,128)(2,1)S(1)} %bitcast.244), channel_id=1, source_target_pairs={{0,2},{2,4},{4,6},{6,8},{8,10},{10,12},{12,14},{14,16},{16,18},{18... | collective-permute-start | bytes 786440 | tf_op jit(solution)/shard_map/ppermute | solution.py:12
  46.1 0.1 copy.102
  46.2 0.3 copy.188
  46.4 11.6 %conditional.1 = (f32[128,4,8]{0,2,1:T(8,128)}, f32[128,4,8]{0,2,1:T(8,128)}, f32[128,4,8,128]{0,3,2,1:T(8,128)S(1)}) conditional(s32[]{:T(128)} %convert_element_type.36, () %tuple.13, (pred[4,8,16]{2,1,0:T(8,128)(4,1)S(1)}, bf16[16,16,4,256]{3,1,0,2:T(8,128)(2,1)}, bf16[128,4,8,128]{3,2,0,1:T(8,128)(2,1)S(1)}) %tuple.72), branch_computations={%region_1.0_spmd, %region_2.6_spmd} | conditional | flops 548946368 | bytes 20634264 | solution.py:69
  46.5 0.1 broadcast_in_dim.79
  46.6 0.1 broadcast_in_dim.80
  46.7 1.7 %bitcast_reduce_fusion = (f32[128,4,8]{0,2,1:T(8,128)S(1)}, f32[4,256,128,8]{2,1,3,0:T(8,128)S(1)}) fusion(pred[4,256]{1,0:T(4,128)(4,1)S(1)} %broadcast_in_dim.80, bf16[128,4,8,128]{3,2,0,1:T(8,128)(2,1)S(1)} %get-tuple-element.32, bf16[256,4,256]{2,0,1:T(8,128)(2,1)} %bitcast), kind=kOutput, calls=%fused_computation.1 | convolution fusion | flops 271577088 | bytes 5522432 | tf_op jit(solution)/shard_map/cond/branch_1_fun/rhgd,khd->rhgk/dot_general | solution.py:20
  48.3 0.6 exponential_multiply_fusion
  49.0 1.7 %fusion.2 = f32[128,4,8]{0,2,1:T(8,128)S(1)} fusion(f32[4,256,128,8]{2,1,3,0:T(8,128)S(1)} %get-tuple-element.56, f32[128,4,8]{0,2,1:T(8,128)} %get-tuple-element.108, pred[4,256]{1,0:T(4,128)(4,1)S(1)} %broadcast_in_dim.80), kind=kLoop, calls=%fused_computation.5 | loop fusion | flops 4190208 | bytes 4228096 | tf_op jit(solution)/shard_map/cond/branch_1_fun/reduce_sum | solution.py:25
  50.7 4.0 %bitcast_add_fusion = f32[128,4,8,128]{3,0,2,1:T(8,128)} fusion(f32[4,256,128,8]{2,1,3,0:T(8,128)S(1)} %get-tuple-element.56, f32[128,4,8]{0,2,1:T(8,128)} %get-tuple-element.108, pred[4,256]{1,0:T(4,128)(4,1)S(1)} %broadcast_in_dim.80, f32[128,4,8]{0,2,1:T(8,128)S(1)} %get-tuple-element.34, bf16[256,4,256]{2,0,1:T(8,128)(2,1)} %bitcast), kind=kOutput, calls=%fused_computation.7 | convolution fusion | flops 273154048 | bytes 6587392 | tf_op jit(solution)/shard_map/cond/branch_1_fun/rhgk,khd->rhgd/dot_general | solution.py:27
  54.7 1.9 %copy.187 = f32[128,4,8,128]{0,3,2,1:T(8,128)S(1)} copy(f32[128,4,8,128]{3,0,2,1:T(8,128)} %bitcast_add_fusion) | data formatting | bytes 4194304 | tf_op jit(solution)/shard_map/cond | solution.py:69
  56.7 1.3 fusion.15
  58.0 1.2 fusion.90
  59.2 1.9 %collective-permute-start.1 = (bf16[128,4,256]{2,0,1:T(8,128)(2,1)S(1)}, bf16[128,4,256]{2,0,1:T(8,128)(2,1)S(1)}, u32[]{:S(2)}, u32[]{:S(2)}) collective-permute-start(bf16[128,4,256]{2,0,1:T(8,128)(2,1)S(1)} %bitcast.246), channel_id=1, source_target_pairs={{0,4},{2,6},{4,8},{6,10},{8,12},{10,14},{12,16},{14,18},{16,20},{1... | collective-permute-start | bytes 786440 | tf_op jit(solution)/shard_map/ppermute | solution.py:12
  61.1 1.4 fusion.89
  62.5 28.2 %collective-permute-done.1 = bf16[128,4,256]{2,0,1:T(8,128)(2,1)S(1)} collective-permute-done((bf16[128,4,256]{2,0,1:T(8,128)(2,1)S(1)}, bf16[128,4,256]{2,0,1:T(8,128)(2,1)S(1)}, u32[]{:S(2)}, u32[]{:S(2)}) %collective-permute-start.1) | collective-permute-done | bytes 262176 | tf_op jit(solution)/shard_map/ppermute | solution.py:12
  90.7 1.9 %collective-permute-start.2 = (bf16[128,4,256]{2,0,1:T(8,128)(2,1)S(1)}, bf16[128,4,256]{2,0,1:T(8,128)(2,1)S(1)}, u32[]{:S(2)}, u32[]{:S(2)}) collective-permute-start(bf16[128,4,256]{2,0,1:T(8,128)(2,1)S(1)} %bitcast.247), channel_id=1, source_target_pairs={{0,6},{2,8},{4,10},{6,12},{8,14},{10,16},{12,18},{14,20},{16,22},{... | collective-permute-start | bytes 786440 | tf_op jit(solution)/shard_map/ppermute | solution.py:12
  92.6 0.5 fusion.88
  93.0 9.9 %collective-permute-done.2 = bf16[128,4,256]{2,0,1:T(8,128)(2,1)S(1)} collective-permute-done((bf16[128,4,256]{2,0,1:T(8,128)(2,1)S(1)}, bf16[128,4,256]{2,0,1:T(8,128)(2,1)S(1)}, u32[]{:S(2)}, u32[]{:S(2)}) %collective-permute-start.2) | collective-permute-done | bytes 262176 | tf_op jit(solution)/shard_map/ppermute | solution.py:12
  102.9 2.1 %collective-permute-start.3 = (bf16[128,4,256]{2,0,1:T(8,128)(2,1)S(1)}, bf16[128,4,256]{2,0,1:T(8,128)(2,1)S(1)}, u32[]{:S(2)}, u32[]{:S(2)}) collective-permute-start(bf16[128,4,256]{2,0,1:T(8,128)(2,1)S(1)} %bitcast.248), channel_id=1, source_target_pairs={{0,8},{2,10},{4,12},{6,14},{8,16},{10,18},{12,20},{14,22},{16,24},... | collective-permute-start | bytes 786440 | tf_op jit(solution)/shard_map/ppermute | solution.py:12
  105.0 0.5 fusion.87
  105.5 7.1 %collective-permute-done.3 = bf16[128,4,256]{2,0,1:T(8,128)(2,1)S(1)} collective-permute-done((bf16[128,4,256]{2,0,1:T(8,128)(2,1)S(1)}, bf16[128,4,256]{2,0,1:T(8,128)(2,1)S(1)}, u32[]{:S(2)}, u32[]{:S(2)}) %collective-permute-start.3) | collective-permute-done | bytes 262176 | tf_op jit(solution)/shard_map/ppermute | solution.py:12
  112.6 0.5 fusion.86
  113.1 1.4 fusion.85
  114.4 1.4 fusion.84
  115.8 1.4 fusion.83
  117.2 1.4 fusion.82
  118.6 0.7 fusion.80
  119.3 0.3 fusion.26
  119.7 0.5 fusion.59
  120.2 0.3 fusion.42
  120.5 0.3 fusion.40
  120.9 0.3 fusion.38
  121.3 0.3 fusion.36
  121.6 0.3 fusion.34
  122.0 0.3 fusion.32
  122.3 0.3 fusion.30
  122.7 0.3 fusion.28
  123.0 0.8 multiply_add_fusion
  123.8 1.4 fusion.45
  125.2 1.4 fusion.47
  126.6 1.4 fusion.49
  128.0 0.5 fusion.51
  128.5 0.5 fusion.53
  129.0 0.5 fusion.55
  129.5 1.4 fusion.57
  130.9 3.0 %fusion.17 = bf16[128,4,8,128]{0,3,2,1:T(8,128)(2,1)S(1)} fusion(f32[4,128,8,128]{1,3,2,0:T(8,128)S(1)} %fusion.45, f32[4,128,8,128]{1,3,2,0:T(8,128)S(1)} %fusion.47, f32[4,128,8,128]{1,3,2,0:T(8,128)S(1)} %fusion.49, f32[4,128,8,128]{1,3,2,0:T(8,128)S(1)} %fusion.51, f32[4,128,8,128]{1,3,2,0:T(8,128)S(1)} %fusion.53, f32[4,128,8,128]{1,3,2,0:T(8,128)S(1)} %fusion.55, ...), kind=kOutput, calls=%fused_computation.23 | convolution fusion | flops 145752064 | bytes 22331392 | tf_op jit(solution)/shard_map/rhgk,khd->rhgd/dot_general | solution.py:27
  133.9 0.9 copy.134
  134.8 15.2 %all_to_all.51 = bf16[128,4,1024]{2,1,0:T(4,128)(2,1)S(1)} all-to-all(bf16[128,4,1024]{2,1,0:T(4,128)(2,1)S(1)} %copy.134), channel_id=1, replica_groups=mesh['seq'=16,'head'=2] {'head'}, dimensions={0} | all-to-all | bytes 2097152 | tf_op jit(solution)/shard_map/all_to_all | solution.py:92
  150.0 0.3 copy.135
  150.4 1.5 %copy.137 = bf16[64,8,1024]{2,1,0:T(8,128)(2,1)} copy(bf16[64,8,1024]{2,0,1:T(8,128)(2,1)S(1)} %bitcast.239) | data formatting | bytes 2097152 | tf_op jit(solution)/shard_map/all_to_all | solution.py:92
  (17 shorter events, 0.2 us)
Async XLA Ops:
  1.7 9.1 %all-to-all-start.1 = ((bf16[64,8,256]{2,0,1:T(8,128)(2,1)}), bf16[64,8,256]{2,0,1:T(8,128)(2,1)S(1)}, u32[]{:S(2)}, u32[]{:S(2)}) async-start(bf16[64,8,256]{2,0,1:T(8,128)(2,1)} %copy.104), calls=%async_computation.1 | async-start | bytes 524288 | tf_op jit(solution)/shard_map/all_to_all | solution.py:37
  8.0 7.0 %copy-start = (bf16[1,16,4,256]{3,2,1,0:T(4,128)(2,1)S(1)}, bf16[1,16,4,256]{3,2,1,0:T(4,128)(2,1)}, u32[]{:S(2)}) copy-start(bf16[1,16,4,256]{3,2,1,0:T(4,128)(2,1)} %param.10) | copy-start | bytes 98308
  10.8 35.3 %all-to-all-start = ((bf16[64,8,1024]{2,0,1:T(8,128)(2,1)}), bf16[64,8,1024]{2,0,1:T(8,128)(2,1)S(1)}, u32[]{:S(2)}, u32[]{:S(2)}) async-start(bf16[64,8,1024]{2,0,1:T(8,128)(2,1)} %copy.101), calls=%async_computation | async-start | bytes 2097152 | tf_op jit(solution)/shard_map/all_to_all | solution.py:36
  35.6 81.6 %collective-permute-start.7 = (bf16[128,4,256]{2,0,1:T(8,128)(2,1)S(1)}, bf16[128,4,256]{2,0,1:T(8,128)(2,1)}, u32[]{:S(2)}, u32[]{:S(2)}) collective-permute-start(bf16[128,4,256]{2,0,1:T(8,128)(2,1)S(1)} %bitcast.240), channel_id=1, source_target_pairs={{0,16},{2,18},{4,20},{6,22},{8,24},{10,26},{12,28},{14,30},{1,17},... | collective-permute-start | bytes 786440 | tf_op jit(solution)/shard_map/ppermute | solution.py:12
  36.9 78.9 %collective-permute-start.6 = (bf16[128,4,256]{2,0,1:T(8,128)(2,1)S(1)}, bf16[128,4,256]{2,0,1:T(8,128)(2,1)}, u32[]{:S(2)}, u32[]{:S(2)}) collective-permute-start(bf16[128,4,256]{2,0,1:T(8,128)(2,1)S(1)} %bitcast.241), channel_id=1, source_target_pairs={{0,14},{2,16},{4,18},{6,20},{8,22},{10,24},{12,26},{14,28},{16,30}... | collective-permute-start | bytes 786440 | tf_op jit(solution)/shard_map/ppermute | solution.py:12
  38.2 76.2 %collective-permute-start.5 = (bf16[128,4,256]{2,0,1:T(8,128)(2,1)S(1)}, bf16[128,4,256]{2,0,1:T(8,128)(2,1)}, u32[]{:S(2)}, u32[]{:S(2)}) collective-permute-start(bf16[128,4,256]{2,0,1:T(8,128)(2,1)S(1)} %bitcast.242), channel_id=1, source_target_pairs={{0,12},{2,14},{4,16},{6,18},{8,20},{10,22},{12,24},{14,26},{16,28}... | collective-permute-start | bytes 786440 | tf_op jit(solution)/shard_map/ppermute | solution.py:12
  42.2 70.8 %collective-permute-start.4 = (bf16[128,4,256]{2,0,1:T(8,128)(2,1)S(1)}, bf16[128,4,256]{2,0,1:T(8,128)(2,1)}, u32[]{:S(2)}, u32[]{:S(2)}) collective-permute-start(bf16[128,4,256]{2,0,1:T(8,128)(2,1)S(1)} %bitcast.243), channel_id=1, source_target_pairs={{0,10},{2,12},{4,14},{6,16},{8,18},{10,20},{12,22},{14,24},{16,26}... | collective-permute-start | bytes 786440 | tf_op jit(solution)/shard_map/ppermute | solution.py:12
  44.1 15.0 %collective-permute-start = (bf16[128,4,256]{2,0,1:T(8,128)(2,1)S(1)}, bf16[128,4,256]{2,0,1:T(8,128)(2,1)}, u32[]{:S(2)}, u32[]{:S(2)}) collective-permute-start(bf16[128,4,256]{2,0,1:T(8,128)(2,1)S(1)} %bitcast.244), channel_id=1, source_target_pairs={{0,2},{2,4},{4,6},{6,8},{8,10},{10,12},{12,14},{14,16},{16,18},{18... | collective-permute-start | bytes 786440 | tf_op jit(solution)/shard_map/ppermute | solution.py:12
  59.2 31.5 %collective-permute-start.1 = (bf16[128,4,256]{2,0,1:T(8,128)(2,1)S(1)}, bf16[128,4,256]{2,0,1:T(8,128)(2,1)S(1)}, u32[]{:S(2)}, u32[]{:S(2)}) collective-permute-start(bf16[128,4,256]{2,0,1:T(8,128)(2,1)S(1)} %bitcast.246), channel_id=1, source_target_pairs={{0,4},{2,6},{4,8},{6,10},{8,12},{10,14},{12,16},{14,18},{16,20},{1... | collective-permute-start | bytes 786440 | tf_op jit(solution)/shard_map/ppermute | solution.py:12
  90.7 12.3 %collective-permute-start.2 = (bf16[128,4,256]{2,0,1:T(8,128)(2,1)S(1)}, bf16[128,4,256]{2,0,1:T(8,128)(2,1)S(1)}, u32[]{:S(2)}, u32[]{:S(2)}) collective-permute-start(bf16[128,4,256]{2,0,1:T(8,128)(2,1)S(1)} %bitcast.247), channel_id=1, source_target_pairs={{0,6},{2,8},{4,10},{6,12},{8,14},{10,16},{12,18},{14,20},{16,22},{... | collective-permute-start | bytes 786440 | tf_op jit(solution)/shard_map/ppermute | solution.py:12
  102.9 9.6 %collective-permute-start.3 = (bf16[128,4,256]{2,0,1:T(8,128)(2,1)S(1)}, bf16[128,4,256]{2,0,1:T(8,128)(2,1)S(1)}, u32[]{:S(2)}, u32[]{:S(2)}) collective-permute-start(bf16[128,4,256]{2,0,1:T(8,128)(2,1)S(1)} %bitcast.248), channel_id=1, source_target_pairs={{0,8},{2,10},{4,12},{6,14},{8,16},{10,18},{12,20},{14,22},{16,24},... | collective-permute-start | bytes 786440 | tf_op jit(solution)/shard_map/ppermute | solution.py:12
where the time goes:
time: 155 us; the launch traced here: 152 us
  waiting for transfers between devices  45.1 us (29%)
  blocking collectives  34.8 us (22%)
  matrix products  25.7 us (17%)
  starting transfers between devices  23.3 us (15%)
  other arithmetic  12 us (8%)
  local copies, waits for them, and re-layouts  9.76 us (6%)
    ppermute x8, waiting for transfers between devices, passed_along(): return lax.ppermute(value, axis, pairs)  45.1 us
    all_gather x1, blocking collectives, per_device(): piece = lax.all_gather(pool, 'seq', axis=0, tiled=True)  19.7 us
    ppermute x8, starting transfers between devices, passed_along(): return lax.ppermute(value, axis, pairs)  16.3 us
    all_to_all x1, blocking collectives, per_device(): lax.all_to_all(mixed, 'head', split_axis=0, concat_axis=1, tiled=True)  15.2 us
    dot_general x10, matrix products, blend_keys(): jnp.einsum('rhgk,khd->rhgd', rounded, value_rows, preferred_element_type=...  14.5 us
    dot_general x10, matrix products, blend_keys(): jnp.einsum('rhgd,khd->rhgk', query, keys, preferred_element_type=jnp.floa...  11.1 us
    reduce_sum x10, other arithmetic, blend_keys(): total = total * factor + jnp.sum(weights, axis=-1)  4.84 us
    unnamed x6, local copies, waits for them, and re-layouts  4.75 us
  transfers between devices with their start and end apart: 10, of which 3 were waited for; matrix products, arithmetic and copies ran while one was open for 17% of the time, Pallas kernels for 0%

commit v1 on v0

--- a/solution.py
+++ b/solution.py
@@ -1,10 +1,14 @@
+import functools
+
 import jax
 import jax.numpy as jnp
 from jax import lax
+from jax.experimental import pallas as pl
+from jax.experimental.pallas import tpu as pltpu
 from jax.sharding import PartitionSpec as P
 
 HEAD_DIM = 128
-
+MESH = pl.DeviceIdType.MESH
 
 def passed_along(value, axis, by):
     count = lax.axis_size(axis)
@@ -92,9 +96,442 @@
     return lax.all_to_all(mixed, "head", split_axis=0, concat_axis=1, tiled=True)
 
 
+PLANES = 4
+PLANE_BLOCKS = 8
+PIECES = 4
+KZ, KX, KY, KD, KSZ, KSX, KSY, KSD = range(8)
+
+
+def relay_kernel(
+    listed,
+    query_ref, pairs_ref, start_ref, pool_ref, table_ref, out_ref,
+    window, prefix, tables, bias, pool_bias,
+    send_sem, recv_sem, pool_send, pool_recv,
+):
+    heads, rows, width = pairs_ref.shape
+    page_rows = pool_ref.shape[1]
+    piece = heads // PIECES
+    seq = lax.axis_index("seq")
+    y = lax.axis_index("head")
+    z, x, c = seq // 4, (seq // 2) % 2, seq % 2
+    place = x * 4 + c * 2 + y
+
+    def device(dz=0, dx=0, dc=0, dy=0):
+        nx = 1 - x if dx else x
+        nc = 1 - c if dc else c
+        ny = 1 - y if dy else y
+        return (((z + dz) * 2 + nx) * 2 + nc, ny)
+
+    up, down = device(dz=1), device(dz=-1)
+    xn, yn, sib = device(dx=1), device(dy=1), device(dc=1)
+
+    barrier = pltpu.get_barrier_semaphore()
+    for other in (xn, yn, sib):
+        pl.semaphore_signal(barrier, inc=1, device_id=other, device_id_type=MESH)
+
+    @pl.when(z < PLANES - 1)
+    def _():
+        pl.semaphore_signal(barrier, inc=1, device_id=up, device_id_type=MESH)
+
+    @pl.when(z > 0)
+    def _():
+        pl.semaphore_signal(barrier, inc=1, device_id=down, device_id_type=MESH)
+
+    def block_at(k, bx, bc, by):
+        return (2 - k) * PLANE_BLOCKS + bx * 4 + bc * 2 + by
+
+    window[:, pl.ds(block_at(0, x, c, y), 1)] = pairs_ref[...][:, None]
+    half = heads // 2
+    own_page = pl.ds(pl.multiple_of(((c * PLANES + z) * 2 + x) * page_rows, page_rows), page_rows)
+    prefix[pl.ds(y * half, half), own_page, :] = pool_ref[...]
+    tables[pl.ds(y, 1)] = table_ref[...][None]
+
+    pl.semaphore_wait(
+        barrier, 3 + jnp.where(z < PLANES - 1, 1, 0) + jnp.where(z > 0, 1, 0)
+    )
+
+    def message(kind, k, j, k_from, bx, bc, by, target):
+        part = pl.ds(j * piece, piece)
+        return pltpu.make_async_remote_copy(
+            src_ref=window.at[part, block_at(k_from, bx, bc, by)],
+            dst_ref=window.at[part, block_at(k, bx, bc, by)],
+            send_sem=send_sem.at[kind, k, j],
+            recv_sem=recv_sem.at[kind, k, j],
+            device_id=target,
+            device_id_type=MESH,
+        )
+
+    source = {
+        KZ: (x, c, y), KX: (x, c, y), KY: (x, c, y),
+        KSZ: (x, c, y), KSX: (1 - x, c, y), KSY: (x, c, 1 - y), KSD: (1 - x, c, 1 - y),
+    }
+    landing = {
+        KZ: (x, c, y), KX: (1 - x, c, y), KY: (x, c, 1 - y), KD: (1 - x, c, 1 - y),
+        KSZ: (x, 1 - c, y), KSX: (1 - x, 1 - c, y),
+        KSY: (x, 1 - c, 1 - y), KSD: (1 - x, 1 - c, 1 - y),
+    }
+    targets = {KZ: up, KX: xn, KY: yn, KSZ: sib, KSX: sib, KSY: sib, KSD: sib}
+
+    def x_first(j):
+        return j < PIECES // 2
+
+    def outgoing(kind, k, j):
+        return message(kind, k, j, k - 1 if kind == KZ else k, *source[kind], targets[kind])
+
+    def corner_out(k, j, by_y):
+        where, target = ((1 - x, c, y), yn) if by_y else ((x, c, 1 - y), xn)
+        return message(KD, k, j, k, *where, target)
+
+    def present(k):
+        return z >= k
+
+    def takes_x(k):
+        if k == 0:
+            return x == 1
+        return present(k) if k == 1 else present(k) & (x == 0)
+
+    def gives_x(k):
+        if k == 0:
+            return x == 0
+        return present(k) if k == 1 else present(k) & (x == 1)
+
+    def sends(kind, k):
+        if kind == KZ:
+            return (z < PLANES - 1) & (z >= k - 1)
+        if kind == KX:
+            return gives_x(k)
+        if kind in (KY, KSZ, KSY):
+            return present(k)
+        return takes_x(k)
+
+    def receives(kind, k):
+        if kind in (KX, KD, KSX, KSD):
+            return takes_x(k)
+        return present(k)
+
+    def corner_sends(k, j, by_y):
+        return takes_x(k) & x_first(j) if by_y else gives_x(k) & jnp.logical_not(x_first(j))
+
+    started = []
+
+    def start(kind, k, j):
+        started.append((kind, k))
+
+        @pl.when(sends(kind, k))
+        def _():
+            outgoing(kind, k, j).start()
+
+    def corner_start(k, j, by_y):
+        @pl.when(corner_sends(k, j, by_y))
+        def _():
+            corner_out(k, j, by_y).start()
+
+    def for_pieces(body):
+        lax.fori_loop(0, PIECES, lambda j, carry: (body(j), carry)[1], 0)
+
+    def arrived(kind, k, j):
+        @pl.when(receives(kind, k))
+        def _():
+            message(kind, k, j, k, *landing[kind], sib).wait_recv()
+
+    def pool_message(index, src, target):
+        return pltpu.make_async_remote_copy(
+            src_ref=src, dst_ref=src,
+            send_sem=pool_send.at[index], recv_sem=pool_recv.at[index],
+            device_id=target, device_id_type=MESH,
+        )
+
+    def layer_at(plane, layer):
+        return prefix.at[
+            :, pl.ds(pl.multiple_of((layer * PLANES + plane) * 2 * page_rows, 2 * page_rows), 2 * page_rows), :
+        ]
+
+    table_out = pool_message(0, tables.at[pl.ds(y, 1)], yn)
+    table_in = pool_message(0, tables.at[pl.ds(1 - y, 1)], yn)
+    py_out = pool_message(1, prefix.at[pl.ds(y * half, half), own_page, :], yn)
+    py_in = pool_message(1, prefix.at[pl.ds((1 - y) * half, half), own_page, :], yn)
+    x_page = pl.ds(pl.multiple_of(((c * PLANES + z) * 2 + 1 - x) * page_rows, page_rows), page_rows)
+    px_out = pool_message(2, prefix.at[:, own_page, :], xn)
+    px_in = pool_message(2, prefix.at[:, x_page, :], xn)
+    UP, DOWN, SIB_UP, SIB_DOWN, SIB_OWN = 3, 6, 9, 12, 15
+
+    def from_below(d):
+        return z >= d
+
+    def from_above(d):
+        return z + d < PLANES
+
+    def up_out(d):
+        return pool_message(UP + d - 1, layer_at(z - d + 1, c), up)
+
+    def down_out(d):
+        return pool_message(DOWN + d - 1, layer_at(z + d - 1, c), down)
+
+    def up_sends(d):
+        return (z < PLANES - 1) & (z >= d - 1)
+
+    def down_sends(d):
+        return (z > 0) & (z + d - 1 < PLANES)
+
+    def pool_start(d):
+        @pl.when(up_sends(d))
+        def _():
+            up_out(d).start()
+
+        @pl.when(down_sends(d))
+        def _():
+            down_out(d).start()
+
+    def pool_arrived(d):
+        @pl.when(from_below(d))
+        def _():
+            pool_message(UP + d - 1, layer_at(z - d, c), up).wait_recv()
+            pool_message(SIB_UP + d - 1, layer_at(z - d, c), sib).start()
+
+        @pl.when(from_above(d))
+        def _():
+            pool_message(DOWN + d - 1, layer_at(z + d, c), up).wait_recv()
+            pool_message(SIB_DOWN + d - 1, layer_at(z + d, c), sib).start()
+
+        if d < PLANES - 1:
+            pool_start(d + 1)
+
+    py_out.start()
+    table_out.start()
+
+    @for_pieces
+    def _(j):
+        for kind, k in ((KZ, 1), (KX, 0), (KY, 0), (KSZ, 0)):
+            start(kind, k, j)
+
+    plane_rows = PLANE_BLOCKS * rows
+
+    @pl.when(z < 2)
+    def _():
+        window[:, :PLANE_BLOCKS] = jnp.zeros((heads, PLANE_BLOCKS, rows, width), window.dtype)
+
+    @pl.when(z < 1)
+    def _():
+        window[:, PLANE_BLOCKS:2 * PLANE_BLOCKS] = jnp.zeros((heads, PLANE_BLOCKS, rows, width), window.dtype)
+
+    span = bias.shape[1]
+    column = lax.broadcasted_iota(jnp.int32, (rows, span), 1)
+    row = lax.broadcasted_iota(jnp.int32, (rows, span), 0)
+    base = (z * PLANE_BLOCKS + place) * rows - 2 * plane_rows
+    seen = (column >= start_ref[...] - base) & (column <= row + 2 * plane_rows)
+    bias[...] = jnp.where(seen, 0.0, -1e30)
+
+    py_in.wait_recv()
+    px_out.start()
+
+    @for_pieces
+    def _(j):
+        arrived(KZ, 1, j)
+        for kind, k in ((KZ, 2), (KX, 1), (KY, 1), (KSZ, 1)):
+            start(kind, k, j)
+
+    px_in.wait_recv()
+    pool_start(1)
+    pool_message(SIB_OWN, layer_at(z, c), sib).start()
+
+    def cross(k, j):
+        arrived(KX, k, j)
+        corner_start(k, j, True)
+        start(KSX, k, j)
+        arrived(KY, k, j)
+        corner_start(k, j, False)
+        start(KSY, k, j)
+
+    def corner(k, j):
+        arrived(KD, k, j)
+        start(KSD, k, j)
+
+    @for_pieces
+    def _(j):
+        cross(0, j)
+
+    @for_pieces
+    def _(j):
+        arrived(KZ, 2, j)
+        for kind, k in ((KX, 2), (KY, 2), (KSZ, 2)):
+            start(kind, k, j)
+
+    pool_arrived(1)
+
+    @for_pieces
+    def _(j):
+        cross(1, j)
+        corner(0, j)
+
+    pool_arrived(2)
+
+    @for_pieces
+    def _(j):
+        cross(2, j)
+        corner(1, j)
+
+    pool_arrived(3)
+
+    @for_pieces
+    def _(j):
+        corner(2, j)
+
+    table_in.wait_recv()
+    pages = PLANES * 4
+    keys = pages * page_rows
+    slot = lax.broadcasted_iota(jnp.int32, (8, keys), 1) // page_rows
+    page = (slot % (pages // 2)) * 2 + slot // (pages // 2)
+    for side in range(2):
+        table = tables[side]
+        chosen = table[:, 0:1] == page
+        for i in range(1, listed):
+            chosen = chosen | (table[:, i:i + 1] == page)
+        mask = jnp.where(chosen, 0.0, -1e30)
+        for i in range(half):
+            pool_bias[side * half + i] = mask[i:i + 1]
+
+    for d in range(1, PLANES):
+        @pl.when(from_below(d))
+        def _():
+            pool_message(SIB_UP + d - 1, layer_at(z - d, 1 - c), sib).wait_recv()
+
+        @pl.when(from_above(d))
+        def _():
+            pool_message(SIB_DOWN + d - 1, layer_at(z + d, 1 - c), sib).wait_recv()
+    pool_message(SIB_OWN, layer_at(z, 1 - c), sib).wait_recv()
+
+    @for_pieces
+    def _(j):
+        for k in range(3):
+            for kind in (KSZ, KSX, KSY, KSD):
+                arrived(kind, k, j)
+
+    factor = HEAD_DIM ** (-0.5) * 1.4426950408889634
+    group = query_ref.shape[2] // HEAD_DIM
+    ones = jnp.ones((span, HEAD_DIM), jnp.bfloat16)
+    pool_ones = jnp.ones((keys, HEAD_DIM), jnp.bfloat16)
+    contract = (((1,), (1,)), ((), ()))
+
+    def one_head(h, carry):
+        queries = query_ref[h]
+        query = jnp.concatenate(
+            [queries[:, g * HEAD_DIM:(g + 1) * HEAD_DIM] for g in range(group)], axis=0
+        )
+        near = window[h, pl.ds(place, 2 * PLANE_BLOCKS + 1)].reshape(span, width)
+        far = prefix[h]
+        near_scores = lax.dot_general(
+            query, near[:, :HEAD_DIM], contract, preferred_element_type=jnp.float32
+        )
+        near_scores = (near_scores.reshape(group, rows, span) + bias[...][None]).reshape(group * rows, span)
+        far_scores = lax.dot_general(
+            query, far[:, :HEAD_DIM], contract, preferred_element_type=jnp.float32
+        )
+        far_scores = far_scores + pool_bias[h]
+        top = jnp.maximum(
+            jnp.max(near_scores, axis=1, keepdims=True), jnp.max(far_scores, axis=1, keepdims=True)
+        )
+        near_weights = jnp.exp2((near_scores - top) * factor).astype(jnp.bfloat16)
+        far_weights = jnp.exp2((far_scores - top) * factor).astype(jnp.bfloat16)
+        mixed = jnp.dot(
+            near_weights,
+            jnp.concatenate([near[:, HEAD_DIM:], ones], axis=1),
+            preferred_element_type=jnp.float32,
+        ) + jnp.dot(
+            far_weights,
+            jnp.concatenate([far[:, HEAD_DIM:], pool_ones], axis=1),
+            preferred_element_type=jnp.float32,
+        )
+        result = (mixed[:, :HEAD_DIM] / mixed[:, HEAD_DIM:]).astype(out_ref.dtype)
+        for g in range(group):
+            out_ref[h, :, g * HEAD_DIM:(g + 1) * HEAD_DIM] = result[g * rows:(g + 1) * rows]
+        return carry
+
+    lax.fori_loop(0, heads, one_head, 0)
+
+    @for_pieces
+    def _(j):
+        for kind, k in started:
+            @pl.when(sends(kind, k))
+            def _():
+                outgoing(kind, k, j).wait_send()
+
+        for k in range(3):
+            for by_y in (True, False):
+                @pl.when(corner_sends(k, j, by_y))
+                def _():
+                    corner_out(k, j, by_y).wait_send()
+
+    table_out.wait_send()
+    py_out.wait_send()
+    px_out.wait_send()
+    pool_message(SIB_OWN, layer_at(z, c), sib).wait_send()
+    for d in range(1, PLANES):
+        @pl.when(up_sends(d))
+        def _():
+            up_out(d).wait_send()
+
+        @pl.when(down_sends(d))
+        def _():
+            down_out(d).wait_send()
+
+        @pl.when(from_below(d))
+        def _():
+            pool_message(SIB_UP + d - 1, layer_at(z - d, c), sib).wait_send()
+
+        @pl.when(from_above(d))
+        def _():
+            pool_message(SIB_DOWN + d - 1, layer_at(z + d, c), sib).wait_send()
+
+
+def relayed(queries, branch_key_value, branch_ids, pool, page_table):
+    rows, heads, width = branch_key_value.shape
+    wide = queries.shape[2]
+    page_rows = pool.shape[1]
+    block = lax.axis_index("seq") * 2 + lax.axis_index("head")
+    own_ids = lax.dynamic_slice_in_dim(branch_ids, block * rows, rows, 0)
+    starts = jnp.sum((branch_ids[None, :] < own_ids[:, None]).astype(jnp.int32), axis=1, keepdims=True)
+    table = jnp.pad(page_table, ((0, 8 - page_table.shape[0]), (0, 128 - page_table.shape[1])))
+    span = 2 * PLANE_BLOCKS * rows + rows
+    pool_keys = PLANES * 4 * page_rows
+    vmem = pl.BlockSpec(memory_space=pltpu.VMEM)
+    attended = pl.pallas_call(
+        functools.partial(relay_kernel, page_table.shape[1]),
+        out_shape=jax.ShapeDtypeStruct((heads, rows, wide), jnp.bfloat16),
+        in_specs=[vmem] * 5,
+        out_specs=vmem,
+        scratch_shapes=[
+            pltpu.VMEM((heads, 3 * PLANE_BLOCKS, rows, width), jnp.bfloat16),
+            pltpu.VMEM((heads, pool_keys, width), jnp.bfloat16),
+            pltpu.VMEM((2, 8, 128), jnp.int32),
+            pltpu.VMEM((rows, span), jnp.float32),
+            pltpu.VMEM((heads, 1, pool_keys), jnp.float32),
+            pltpu.SemaphoreType.DMA((8, 3, PIECES)),
+            pltpu.SemaphoreType.DMA((8, 3, PIECES)),
+            pltpu.SemaphoreType.DMA((16,)),
+            pltpu.SemaphoreType.DMA((16,)),
+        ],
+        compiler_params=pltpu.CompilerParams(
+            collective_id=0, has_side_effects=True, vmem_limit_bytes=48 * 2**20
+        ),
+        cost_estimate=pl.CostEstimate(
+            flops=4 * rows * wide * (span + pool_keys) * heads,
+            bytes_accessed=2 * 2 * heads * rows * wide,
+            transcendentals=rows * heads * (wide // HEAD_DIM) * (span + pool_keys),
+        ),
+    )(
+        jnp.swapaxes(queries, 0, 1),
+        jnp.swapaxes(branch_key_value, 0, 1),
+        starts,
+        jnp.swapaxes(pool[0], 0, 1),
+        table,
+    )
+    return jnp.swapaxes(attended, 0, 1)
+
+
 def solution(mesh):
+    small = mesh.shape["seq"] == PLANES * 4 and mesh.shape["head"] == 2
     return jax.shard_map(
-        per_device,
+        relayed if small else per_device,
         mesh=mesh,
         in_specs=(
             P(("seq", "head"), None, None),

time: 155 us -> 54.9 us (0.35); the launches traced: 152 us -> 54.6 us
  Pallas kernels: 0 us -> 49.1 us
  waiting for transfers between devices: 45.1 us -> 0 us
  blocking collectives: 34.8 us -> 0 us
  matrix products: 25.7 us -> 0 us
  starting transfers between devices: 23.3 us -> 0 us
  other arithmetic: 12 us -> 0.22 us
  local copies, waits for them, and re-layouts: 9.76 us -> 5.23 us
    pallas_call x0 -> x1, Pallas kernels: none -> 49.1 us  [relayed(): pl.pallas_call(functools.partial(relay_kernel, page_table.shape[1]), out_...]
    ppermute x8 -> x0, waiting for transfers between devices: 45.1 us -> none  [passed_along(): return lax.ppermute(value, axis, pairs)]
    dot_general x20 -> x0, matrix products: 25.7 us -> none  [the longest x10 14.5 us: blend_keys(): jnp.einsum('rhgk,khd->rhgd', rounded, value_rows, preferred_element_type=...]
    all_gather x1 -> x0, blocking collectives: 19.7 us -> none  [per_device(): piece = lax.all_gather(pool, 'seq', axis=0, tiled=True)]
    ppermute x8 -> x0, starting transfers between devices: 16.3 us -> none  [passed_along(): return lax.ppermute(value, axis, pairs)]
    all_to_all x1 -> x0, blocking collectives: 15.2 us -> none  [per_device(): lax.all_to_all(mixed, 'head', split_axis=0, concat_axis=1, tiled=True)]
    all_to_all x2 -> x0, starting transfers between devices: 7.02 us -> none  [the longest x1 3.58 us: per_device(): lax.all_to_all(queries, 'head', split_axis=1, concat_axis=0, tiled=True)]
    reduce_sum x10 -> x1, other arithmetic: 4.84 us -> 0.22 us  [relayed(): jnp.sum((branch_ids[None, :] < own_ids[:, None]).astype(jnp.int32), axis=...]
  transfers between devices with their start and end apart: 10 -> 0, of which waited for: 3 -> 0; matrix products, arithmetic and copies ran while one was open for 17% -> 0% of each run, Pallas kernels for 0% -> 0%
where the time goes in v1:
time: 54.9 us; the launch traced here: 54.6 us
  Pallas kernels  49.1 us (89%)
  local copies, waits for them, and re-layouts  5.23 us (10%)
    pallas_call x1, Pallas kernels, relayed(): pl.pallas_call(functools.partial(relay_kernel, page_table.shape[1]), out_...  49.1 us
    unnamed x9, local copies, waits for them, and re-layouts  3.51 us
    transpose x1, local copies, waits for them, and re-layouts, relayed(): return jnp.swapaxes(attended, 0, 1)  1.55 us

profile of v1, /device:TPU:17, one launch (start us, length us, event | category | flops | bytes accessed | tf_op | source)
XLA Modules:
  0.0 54.6 jit_solution(5968018806827737934)
XLA Ops:
  0.0 0.0 copy-start.1
  0.0 0.0 copy-start.2
  0.0 0.0 copy-start
  0.0 0.7 %copy-done.1 = s32[2048]{0:T(1024)S(1)} copy-done((s32[2048]{0:T(1024)S(1)}, s32[2048]{0:T(1024)}, u32[]{:S(2)}) %copy-start.1) | copy-done | bytes 8216
  0.7 0.1 dynamic_slice.3
  0.8 0.2 convert_reduce_fusion
  1.0 0.0 copy-done.2
  1.0 0.1 copy.14.start_ref
  1.1 0.0 copy-done
  1.1 1.0 %copy.20 = bf16[64,8,256]{2,0,1:T(8,128)(2,1)S(1)} copy(bf16[64,8,256]{2,1,0:T(8,128)(2,1)} %param.6) | data formatting | bytes 524288 | tf_op args[1]
  2.1 1.8 %copy.19 = bf16[64,8,1024]{2,0,1:T(8,128)(2,1)S(1)} copy(bf16[64,8,1024]{2,1,0:T(8,128)(2,1)} %param.5) | data formatting | bytes 2097152 | tf_op args[0]
  3.9 49.1 %shard_map.55 = bf16[8,64,1024]{2,1,0:T(8,128)(2,1)S(1)} custom-call(bf16[8,64,1024]{2,1,0:T(8,128)(2,1)S(1)} %bitcast.14, bf16[8,64,256]{2,1,0:T(8,128)(2,1)S(1)} %bitcast.15, s32[64,1]{1,0:T(8,128)S(1)} %copy.14.start_ref, bf16[4,16,256]{2,1,0:T(8,128)(2,1)S(1)} %bitcast.16, s32[8,128]{1,0:T(8,128)S(1)} %pad.4.table_ref), custom_call_target="tpu_custom_call" | custom-call | flops 2818572288 | bytes 2097152 | tf_op jit(solution)/shard_map/pallas_call | solution.py:497
  53.1 1.5 %copy.15 = bf16[64,8,1024]{2,1,0:T(8,128)(2,1)} copy(bf16[64,8,1024]{2,0,1:T(8,128)(2,1)S(1)} %bitcast.13) | data formatting | bytes 2097152 | tf_op jit(solution)/shard_map/transpose | solution.py:528
  (2 shorter events, 0.0 us)
Async XLA Ops:
  0.0 0.7 %copy-start.1 = (s32[2048]{0:T(1024)S(1)}, s32[2048]{0:T(1024)}, u32[]{:S(2)}) copy-start(s32[2048]{0:T(1024)} %param.7) | copy-start | bytes 24580
  0.0 1.0 %copy-start.2 = (s32[4,8]{1,0:T(4,128)S(1)}, s32[4,8]{1,0:T(4,128)}, u32[]{:S(2)}) copy-start(s32[4,8]{1,0:T(4,128)} %param.9) | copy-start | bytes 388
  0.0 1.1 %copy-start = (bf16[1,16,4,256]{3,2,1,0:T(4,128)(2,1)S(1)}, bf16[1,16,4,256]{3,2,1,0:T(4,128)(2,1)}, u32[]{:S(2)}) copy-start(bf16[1,16,4,256]{3,2,1,0:T(4,128)(2,1)} %param.8) | copy-start | bytes 98308

commit v2 on v1

--- a/solution.py
+++ b/solution.py
@@ -105,7 +105,7 @@
 def relay_kernel(
     listed,
     query_ref, pairs_ref, start_ref, pool_ref, table_ref, out_ref,
-    window, prefix, tables, bias, pool_bias,
+    window, prefix, tables, bias, pool_bias, mixed, tops,
     send_sem, recv_sem, pool_send, pool_recv,
 ):
     heads, rows, width = pairs_ref.shape
@@ -367,14 +367,9 @@
 
     @for_pieces
     def _(j):
-        cross(2, j)
         corner(1, j)
 
     pool_arrived(3)
-
-    @for_pieces
-    def _(j):
-        corner(2, j)
 
     table_in.wait_recv()
     pages = PLANES * 4
@@ -400,53 +395,77 @@
             pool_message(SIB_DOWN + d - 1, layer_at(z + d, 1 - c), sib).wait_recv()
     pool_message(SIB_OWN, layer_at(z, 1 - c), sib).wait_recv()
 
-    @for_pieces
-    def _(j):
-        for k in range(3):
-            for kind in (KSZ, KSX, KSY, KSD):
-                arrived(kind, k, j)
-
     factor = HEAD_DIM ** (-0.5) * 1.4426950408889634
     group = query_ref.shape[2] // HEAD_DIM
-    ones = jnp.ones((span, HEAD_DIM), jnp.bfloat16)
-    pool_ones = jnp.ones((keys, HEAD_DIM), jnp.bfloat16)
+    far_span = PLANE_BLOCKS * rows
+    near_span = span - far_span
     contract = (((1,), (1,)), ((), ()))
 
-    def one_head(h, carry):
+    def stacked_queries(h):
         queries = query_ref[h]
-        query = jnp.concatenate(
+        return jnp.concatenate(
             [queries[:, g * HEAD_DIM:(g + 1) * HEAD_DIM] for g in range(group)], axis=0
         )
-        near = window[h, pl.ds(place, 2 * PLANE_BLOCKS + 1)].reshape(span, width)
-        far = prefix[h]
-        near_scores = lax.dot_general(
-            query, near[:, :HEAD_DIM], contract, preferred_element_type=jnp.float32
-        )
-        near_scores = (near_scores.reshape(group, rows, span) + bias[...][None]).reshape(group * rows, span)
-        far_scores = lax.dot_general(
-            query, far[:, :HEAD_DIM], contract, preferred_element_type=jnp.float32
-        )
-        far_scores = far_scores + pool_bias[h]
+
+    def scores_of(query, pairs, mask):
+        scores = lax.dot_general(
+            query, pairs[:, :HEAD_DIM], contract, preferred_element_type=jnp.float32
+        )
+        count = pairs.shape[0]
+        return (scores.reshape(group, rows, count) + mask[None]).reshape(group * rows, count)
+
+    def weighted(scores, top, pairs):
+        weights = jnp.exp2((scores - top) * factor).astype(jnp.bfloat16)
+        values = jnp.concatenate(
+            [pairs[:, HEAD_DIM:], jnp.ones((pairs.shape[0], HEAD_DIM), jnp.bfloat16)], axis=1
+        )
+        return jnp.dot(weights, values, preferred_element_type=jnp.float32)
+
+    def early(h):
+        query = stacked_queries(h)
+        near = window[h, pl.ds(place + PLANE_BLOCKS, PLANE_BLOCKS + 1)].reshape(near_span, width)
+        pool_pairs = prefix[h]
+        near_scores = scores_of(query, near, bias[:, far_span:])
+        pool_scores = scores_of(query, pool_pairs, pool_bias[h])
         top = jnp.maximum(
-            jnp.max(near_scores, axis=1, keepdims=True), jnp.max(far_scores, axis=1, keepdims=True)
-        )
-        near_weights = jnp.exp2((near_scores - top) * factor).astype(jnp.bfloat16)
-        far_weights = jnp.exp2((far_scores - top) * factor).astype(jnp.bfloat16)
-        mixed = jnp.dot(
-            near_weights,
-            jnp.concatenate([near[:, HEAD_DIM:], ones], axis=1),
-            preferred_element_type=jnp.float32,
-        ) + jnp.dot(
-            far_weights,
-            jnp.concatenate([far[:, HEAD_DIM:], pool_ones], axis=1),
-            preferred_element_type=jnp.float32,
-        )
-        result = (mixed[:, :HEAD_DIM] / mixed[:, HEAD_DIM:]).astype(out_ref.dtype)
+            jnp.max(near_scores, axis=1, keepdims=True), jnp.max(pool_scores, axis=1, keepdims=True)
+        )
+        mixed[h] = weighted(near_scores, top, near) + weighted(pool_scores, top, pool_pairs)
+        tops[h] = jnp.broadcast_to(top, tops.shape[1:])
+
+    def late(h):
+        query = stacked_queries(h)
+        far = window[h, pl.ds(place, PLANE_BLOCKS)].reshape(far_span, width)
+        scores = scores_of(query, far, bias[:, :far_span])
+        before = tops[h][:, :1]
+        top = jnp.maximum(before, jnp.max(scores, axis=1, keepdims=True))
+        total = mixed[h] * jnp.exp2((before - top) * factor) + weighted(scores, top, far)
+        result = (total[:, :HEAD_DIM] / total[:, HEAD_DIM:]).astype(out_ref.dtype)
         for g in range(group):
             out_ref[h, :, g * HEAD_DIM:(g + 1) * HEAD_DIM] = result[g * rows:(g + 1) * rows]
-        return carry
-
-    lax.fori_loop(0, heads, one_head, 0)
+
+    def for_heads(j, body):
+        lax.fori_loop(0, piece, lambda i, carry: (body(j * piece + i), carry)[1], 0)
+
+    def from_sibling(k, j):
+        for kind in (KSZ, KSX, KSY, KSD):
+            arrived(kind, k, j)
+
+    @for_pieces
+    def _(j):
+        cross(2, j)
+        from_sibling(0, j)
+        from_sibling(1, j)
+        for_heads(j, early)
+
+    @for_pieces
+    def _(j):
+        corner(2, j)
+
+    @for_pieces
+    def _(j):
+        from_sibling(2, j)
+        for_heads(j, late)
 
     @for_pieces
     def _(j):
@@ -505,6 +524,8 @@
             pltpu.VMEM((2, 8, 128), jnp.int32),
             pltpu.VMEM((rows, span), jnp.float32),
             pltpu.VMEM((heads, 1, pool_keys), jnp.float32),
+            pltpu.VMEM((heads, rows * (wide // HEAD_DIM), 2 * HEAD_DIM), jnp.float32),
+            pltpu.VMEM((heads, rows * (wide // HEAD_DIM), HEAD_DIM), jnp.float32),
             pltpu.SemaphoreType.DMA((8, 3, PIECES)),
             pltpu.SemaphoreType.DMA((8, 3, PIECES)),
             pltpu.SemaphoreType.DMA((16,)),

time: 54.9 us -> 56.2 us (1.024)
  Pallas kernels: 49.1 us -> 50.1 us
    pallas_call x1, Pallas kernels: 49.1 us -> 50.1 us  [relayed(): pl.pallas_call(functools.partial(relay_kernel, page_table.shape[1]), out_...]
where the time goes in v2:
time: 56.2 us; the launch traced here: 55.6 us
  Pallas kernels  50.1 us (89%)
  local copies, waits for them, and re-layouts  5.23 us (9%)
    pallas_call x1, Pallas kernels, relayed(): pl.pallas_call(functools.partial(relay_kernel, page_table.shape[1]), out_...  50.1 us
    unnamed x9, local copies, waits for them, and re-layouts  3.51 us
    transpose x1, local copies, waits for them, and re-layouts, relayed(): return jnp.swapaxes(attended, 0, 1)  1.55 us

profile of v2, /device:TPU:17, one launch (start us, length us, event | category | flops | bytes accessed | tf_op | source)
XLA Modules:
  0.0 55.6 jit_solution(13696412802059636344)
XLA Ops:
  0.0 0.0 copy-start.1
  0.0 0.0 copy-start.2
  0.0 0.0 copy-start
  0.0 0.7 %copy-done.1 = s32[2048]{0:T(1024)S(1)} copy-done((s32[2048]{0:T(1024)S(1)}, s32[2048]{0:T(1024)}, u32[]{:S(2)}) %copy-start.1) | copy-done | bytes 8216
  0.7 0.1 dynamic_slice.3
  0.8 0.2 convert_reduce_fusion
  1.0 0.0 copy-done.2
  1.0 0.1 copy.14.start_ref
  1.1 0.0 copy-done
  1.1 1.0 %copy.20 = bf16[64,8,256]{2,0,1:T(8,128)(2,1)S(1)} copy(bf16[64,8,256]{2,1,0:T(8,128)(2,1)} %param.6) | data formatting | bytes 524288 | tf_op args[1]
  2.1 1.8 %copy.19 = bf16[64,8,1024]{2,0,1:T(8,128)(2,1)S(1)} copy(bf16[64,8,1024]{2,1,0:T(8,128)(2,1)} %param.5) | data formatting | bytes 2097152 | tf_op args[0]
  3.9 50.1 %shard_map.55 = bf16[8,64,1024]{2,1,0:T(8,128)(2,1)S(1)} custom-call(bf16[8,64,1024]{2,1,0:T(8,128)(2,1)S(1)} %bitcast.14, bf16[8,64,256]{2,1,0:T(8,128)(2,1)S(1)} %bitcast.15, s32[64,1]{1,0:T(8,128)S(1)} %copy.14.start_ref, bf16[4,16,256]{2,1,0:T(8,128)(2,1)S(1)} %bitcast.16, s32[8,128]{1,0:T(8,128)S(1)} %pad.4.table_ref), custom_call_target="tpu_custom_call" | custom-call | flops 2818572288 | bytes 2097152 | tf_op jit(solution)/shard_map/pallas_call | solution.py:516
  54.0 1.5 %copy.15 = bf16[64,8,1024]{2,1,0:T(8,128)(2,1)} copy(bf16[64,8,1024]{2,0,1:T(8,128)(2,1)S(1)} %bitcast.13) | data formatting | bytes 2097152 | tf_op jit(solution)/shard_map/transpose | solution.py:549
  (2 shorter events, 0.0 us)
Async XLA Ops:
  0.0 0.7 %copy-start.1 = (s32[2048]{0:T(1024)S(1)}, s32[2048]{0:T(1024)}, u32[]{:S(2)}) copy-start(s32[2048]{0:T(1024)} %param.7) | copy-start | bytes 24580
  0.0 1.0 %copy-start.2 = (s32[4,8]{1,0:T(4,128)S(1)}, s32[4,8]{1,0:T(4,128)}, u32[]{:S(2)}) copy-start(s32[4,8]{1,0:T(4,128)} %param.9) | copy-start | bytes 388
  0.0 1.1 %copy-start = (bf16[1,16,4,256]{3,2,1,0:T(4,128)(2,1)S(1)}, bf16[1,16,4,256]{3,2,1,0:T(4,128)(2,1)}, u32[]{:S(2)}) copy-start(bf16[1,16,4,256]{3,2,1,0:T(4,128)(2,1)} %param.8) | copy-start | bytes 98308

commit v3 on v2

--- a/solution.py
+++ b/solution.py
@@ -98,6 +98,7 @@
 
 PLANES = 4
 PLANE_BLOCKS = 8
+CHUNK = 16
 PIECES = 4
 KZ, KX, KY, KD, KSZ, KSX, KSY, KSD = range(8)
 
@@ -105,7 +106,7 @@
 def relay_kernel(
     listed,
     query_ref, pairs_ref, start_ref, pool_ref, table_ref, out_ref,
-    window, prefix, tables, bias, pool_bias, mixed, tops,
+    window, prefix, tables, bias, pool_bias, scores, weights, mixed, tops,
     send_sem, recv_sem, pool_send, pool_recv,
 ):
     heads, rows, width = pairs_ref.shape
@@ -407,40 +408,53 @@
             [queries[:, g * HEAD_DIM:(g + 1) * HEAD_DIM] for g in range(group)], axis=0
         )
 
-    def scores_of(query, pairs, mask):
-        scores = lax.dot_general(
+    def score(query, pairs):
+        scores[:, :pairs.shape[0]] = lax.dot_general(
             query, pairs[:, :HEAD_DIM], contract, preferred_element_type=jnp.float32
         )
+
+    def weighted(pairs):
         count = pairs.shape[0]
-        return (scores.reshape(group, rows, count) + mask[None]).reshape(group * rows, count)
-
-    def weighted(scores, top, pairs):
-        weights = jnp.exp2((scores - top) * factor).astype(jnp.bfloat16)
         values = jnp.concatenate(
-            [pairs[:, HEAD_DIM:], jnp.ones((pairs.shape[0], HEAD_DIM), jnp.bfloat16)], axis=1
+            [pairs[:, HEAD_DIM:], jnp.ones((count, HEAD_DIM), jnp.bfloat16)], axis=1
         )
-        return jnp.dot(weights, values, preferred_element_type=jnp.float32)
+        return jnp.dot(weights[:, :count], values, preferred_element_type=jnp.float32)
+
+    def chunks():
+        for r in range(0, rows, CHUNK):
+            for g in range(group):
+                yield pl.ds(r, CHUNK), pl.ds(g * rows + r, CHUNK)
 
     def early(h):
-        query = stacked_queries(h)
         near = window[h, pl.ds(place + PLANE_BLOCKS, PLANE_BLOCKS + 1)].reshape(near_span, width)
-        pool_pairs = prefix[h]
-        near_scores = scores_of(query, near, bias[:, far_span:])
-        pool_scores = scores_of(query, pool_pairs, pool_bias[h])
-        top = jnp.maximum(
-            jnp.max(near_scores, axis=1, keepdims=True), jnp.max(pool_scores, axis=1, keepdims=True)
-        )
-        mixed[h] = weighted(near_scores, top, near) + weighted(pool_scores, top, pool_pairs)
-        tops[h] = jnp.broadcast_to(top, tops.shape[1:])
+        pairs = jnp.concatenate([prefix[h], near], axis=0)
+        score(stacked_queries(h), pairs)
+        count = keys + near_span
+        for mask_rows, own in chunks():
+            pool_scores = scores[own, :keys] + pool_bias[h]
+            near_scores = scores[own, keys:count] + bias[mask_rows, far_span:]
+            top = factor * jnp.maximum(
+                jnp.max(pool_scores, axis=1, keepdims=True), jnp.max(near_scores, axis=1, keepdims=True)
+            )
+            weights[own, :keys] = jnp.exp2(pool_scores * factor - top).astype(jnp.bfloat16)
+            weights[own, keys:count] = jnp.exp2(near_scores * factor - top).astype(jnp.bfloat16)
+            tops[h, own] = jnp.broadcast_to(top, (CHUNK, HEAD_DIM))
+        mixed[h] = weighted(pairs)
 
     def late(h):
-        query = stacked_queries(h)
         far = window[h, pl.ds(place, PLANE_BLOCKS)].reshape(far_span, width)
-        scores = scores_of(query, far, bias[:, :far_span])
-        before = tops[h][:, :1]
-        top = jnp.maximum(before, jnp.max(scores, axis=1, keepdims=True))
-        total = mixed[h] * jnp.exp2((before - top) * factor) + weighted(scores, top, far)
-        result = (total[:, :HEAD_DIM] / total[:, HEAD_DIM:]).astype(out_ref.dtype)
+        score(stacked_queries(h), far)
+        for mask_rows, own in chunks():
+            far_scores = scores[own, :far_span] + bias[mask_rows, :far_span]
+            before = tops[h, own]
+            top = jnp.maximum(before, factor * jnp.max(far_scores, axis=1, keepdims=True))
+            weights[own, :far_span] = jnp.exp2(far_scores * factor - top[:, :1]).astype(jnp.bfloat16)
+            tops[h, own] = jnp.exp2(before - top)
+        part = weighted(far)
+        shrink = tops[h]
+        value_sum = mixed[h, :, :HEAD_DIM] * shrink + part[:, :HEAD_DIM]
+        total = mixed[h, :, HEAD_DIM:] * shrink + part[:, HEAD_DIM:]
+        result = (value_sum / total).astype(out_ref.dtype)
         for g in range(group):
             out_ref[h, :, g * HEAD_DIM:(g + 1) * HEAD_DIM] = result[g * rows:(g + 1) * rows]
 
@@ -524,6 +538,8 @@
             pltpu.VMEM((2, 8, 128), jnp.int32),
             pltpu.VMEM((rows, span), jnp.float32),
             pltpu.VMEM((heads, 1, pool_keys), jnp.float32),
+            pltpu.VMEM((rows * (wide // HEAD_DIM), pool_keys + (PLANE_BLOCKS + 1) * rows), jnp.float32),
+            pltpu.VMEM((rows * (wide // HEAD_DIM), pool_keys + (PLANE_BLOCKS + 1) * rows), jnp.bfloat16),
             pltpu.VMEM((heads, rows * (wide // HEAD_DIM), 2 * HEAD_DIM), jnp.float32),
             pltpu.VMEM((heads, rows * (wide // HEAD_DIM), HEAD_DIM), jnp.float32),
             pltpu.SemaphoreType.DMA((8, 3, PIECES)),

time: 56.2 us -> 58 us (1.032)
  Pallas kernels: 50.1 us -> 51.5 us
    pallas_call x1, Pallas kernels: 50.1 us -> 51.5 us  [relayed(): pl.pallas_call(functools.partial(relay_kernel, page_table.shape[1]), out_...]
where the time goes in v3:
time: 58 us; the launch traced here: 57 us
  Pallas kernels  51.5 us (89%)
  local copies, waits for them, and re-layouts  5.23 us (9%)
    pallas_call x1, Pallas kernels, relayed(): pl.pallas_call(functools.partial(relay_kernel, page_table.shape[1]), out_...  51.5 us
    unnamed x9, local copies, waits for them, and re-layouts  3.51 us
    transpose x1, local copies, waits for them, and re-layouts, relayed(): return jnp.swapaxes(attended, 0, 1)  1.55 us

profile of v3, /device:TPU:17, one launch (start us, length us, event | category | flops | bytes accessed | tf_op | source)
XLA Modules:
  0.0 57.0 jit_solution(3259498261476763029)
XLA Ops:
  0.0 0.0 copy-start.1
  0.0 0.0 copy-start.2
  0.0 0.0 copy-start
  0.0 0.7 %copy-done.1 = s32[2048]{0:T(1024)S(1)} copy-done((s32[2048]{0:T(1024)S(1)}, s32[2048]{0:T(1024)}, u32[]{:S(2)}) %copy-start.1) | copy-done | bytes 8216
  0.7 0.1 dynamic_slice.3
  0.8 0.2 convert_reduce_fusion
  1.0 0.0 copy-done.2
  1.0 0.1 copy.14.start_ref
  1.1 0.0 copy-done
  1.1 1.0 %copy.20 = bf16[64,8,256]{2,0,1:T(8,128)(2,1)S(1)} copy(bf16[64,8,256]{2,1,0:T(8,128)(2,1)} %param.6) | data formatting | bytes 524288 | tf_op args[1]
  2.1 1.8 %copy.19 = bf16[64,8,1024]{2,0,1:T(8,128)(2,1)S(1)} copy(bf16[64,8,1024]{2,1,0:T(8,128)(2,1)} %param.5) | data formatting | bytes 2097152 | tf_op args[0]
  3.9 51.5 %shard_map.55 = bf16[8,64,1024]{2,1,0:T(8,128)(2,1)S(1)} custom-call(bf16[8,64,1024]{2,1,0:T(8,128)(2,1)S(1)} %bitcast.14, bf16[8,64,256]{2,1,0:T(8,128)(2,1)S(1)} %bitcast.15, s32[64,1]{1,0:T(8,128)S(1)} %copy.14.start_ref, bf16[4,16,256]{2,1,0:T(8,128)(2,1)S(1)} %bitcast.16, s32[8,128]{1,0:T(8,128)S(1)} %pad.4.table_ref), custom_call_target="tpu_custom_call" | custom-call | flops 2818572288 | bytes 2097152 | tf_op jit(solution)/shard_map/pallas_call | solution.py:530
  55.4 1.5 %copy.15 = bf16[64,8,1024]{2,1,0:T(8,128)(2,1)} copy(bf16[64,8,1024]{2,0,1:T(8,128)(2,1)S(1)} %bitcast.13) | data formatting | bytes 2097152 | tf_op jit(solution)/shard_map/transpose | solution.py:565
  (2 shorter events, 0.0 us)
Async XLA Ops:
  0.0 0.7 %copy-start.1 = (s32[2048]{0:T(1024)S(1)}, s32[2048]{0:T(1024)}, u32[]{:S(2)}) copy-start(s32[2048]{0:T(1024)} %param.7) | copy-start | bytes 24580
  0.0 1.0 %copy-start.2 = (s32[4,8]{1,0:T(4,128)S(1)}, s32[4,8]{1,0:T(4,128)}, u32[]{:S(2)}) copy-start(s32[4,8]{1,0:T(4,128)} %param.9) | copy-start | bytes 388
  0.0 1.1 %copy-start = (bf16[1,16,4,256]{3,2,1,0:T(4,128)(2,1)S(1)}, bf16[1,16,4,256]{3,2,1,0:T(4,128)(2,1)}, u32[]{:S(2)}) copy-start(bf16[1,16,4,256]{3,2,1,0:T(4,128)(2,1)} %param.8) | copy-start | bytes 98308

commit v4 on v3

--- a/solution.py
+++ b/solution.py
@@ -99,7 +99,7 @@
 PLANES = 4
 PLANE_BLOCKS = 8
 CHUNK = 16
-PIECES = 4
+PIECES = 2
 KZ, KX, KY, KD, KSZ, KSX, KSY, KSD = range(8)
 
 
@@ -351,14 +351,14 @@
     def _(j):
         cross(0, j)
 
+    pool_arrived(1)
+
     @for_pieces
     def _(j):
         arrived(KZ, 2, j)
         for kind, k in ((KX, 2), (KY, 2), (KSZ, 2)):
             start(kind, k, j)
 
-    pool_arrived(1)
-
     @for_pieces
     def _(j):
         cross(1, j)
@@ -372,9 +372,86 @@
 
     pool_arrived(3)
 
+    factor = HEAD_DIM ** (-0.5) * 1.4426950408889634
+    group = query_ref.shape[2] // HEAD_DIM
+    keys = PLANES * 4 * page_rows
+    far_span = PLANE_BLOCKS * rows
+    near_span = span - far_span
+    contract = (((1,), (1,)), ((), ()))
+
+    def stacked_queries(h):
+        queries = query_ref[h]
+        return jnp.concatenate(
+            [queries[:, g * HEAD_DIM:(g + 1) * HEAD_DIM] for g in range(group)], axis=0
+        )
+
+    def score(query, pairs):
+        scores[:, :pairs.shape[0]] = lax.dot_general(
+            query, pairs[:, :HEAD_DIM], contract, preferred_element_type=jnp.float32
+        )
+
+    def weighted(pairs):
+        count = pairs.shape[0]
+        values = jnp.concatenate(
+            [pairs[:, HEAD_DIM:], jnp.ones((count, HEAD_DIM), jnp.bfloat16)], axis=1
+        )
+        return jnp.dot(weights[:, :count], values, preferred_element_type=jnp.float32)
+
+    def chunks():
+        for r in range(0, rows, CHUNK):
+            for g in range(group):
+                yield pl.ds(r, CHUNK), pl.ds(g * rows + r, CHUNK)
+
+    def early(h):
+        near = window[h, pl.ds(place + PLANE_BLOCKS, PLANE_BLOCKS + 1)].reshape(near_span, width)
+        score(stacked_queries(h), near)
+        for mask_rows, own in chunks():
+            near_scores = scores[own, :near_span] + bias[mask_rows, far_span:]
+            top = factor * jnp.max(near_scores, axis=1, keepdims=True)
+            weights[own, :near_span] = jnp.exp2(near_scores * factor - top).astype(jnp.bfloat16)
+            tops[h, own] = jnp.broadcast_to(top, (CHUNK, HEAD_DIM))
+        mixed[h] = weighted(near)
+
+    def late(h):
+        far = window[h, pl.ds(place, PLANE_BLOCKS)].reshape(far_span, width)
+        far = jnp.concatenate([prefix[h], far], axis=0)
+        score(stacked_queries(h), far)
+        count = keys + far_span
+        for mask_rows, own in chunks():
+            pool_scores = scores[own, :keys] + pool_bias[h]
+            far_scores = scores[own, keys:count] + bias[mask_rows, :far_span]
+            before = tops[h, own]
+            top = jnp.maximum(
+                jnp.max(pool_scores, axis=1, keepdims=True), jnp.max(far_scores, axis=1, keepdims=True)
+            )
+            top = jnp.maximum(before, factor * top)
+            weights[own, :keys] = jnp.exp2(pool_scores * factor - top[:, :1]).astype(jnp.bfloat16)
+            weights[own, keys:count] = jnp.exp2(far_scores * factor - top[:, :1]).astype(jnp.bfloat16)
+            tops[h, own] = jnp.exp2(before - top)
+        part = weighted(far)
+        shrink = tops[h]
+        value_sum = mixed[h, :, :HEAD_DIM] * shrink + part[:, :HEAD_DIM]
+        total = mixed[h, :, HEAD_DIM:] * shrink + part[:, HEAD_DIM:]
+        result = (value_sum / total).astype(out_ref.dtype)
+        for g in range(group):
+            out_ref[h, :, g * HEAD_DIM:(g + 1) * HEAD_DIM] = result[g * rows:(g + 1) * rows]
+
+    def for_heads(j, body):
+        lax.fori_loop(0, piece, lambda i, carry: (body(j * piece + i), carry)[1], 0)
+
+    def from_sibling(k, j):
+        for kind in (KSZ, KSX, KSY, KSD):
+            arrived(kind, k, j)
+
+    @for_pieces
+    def _(j):
+        cross(2, j)
+        from_sibling(0, j)
+        from_sibling(1, j)
+        for_heads(j, early)
+
     table_in.wait_recv()
     pages = PLANES * 4
-    keys = pages * page_rows
     slot = lax.broadcasted_iota(jnp.int32, (8, keys), 1) // page_rows
     page = (slot % (pages // 2)) * 2 + slot // (pages // 2)
     for side in range(2):
@@ -386,6 +463,10 @@
         for i in range(half):
             pool_bias[side * half + i] = mask[i:i + 1]
 
+    @for_pieces
+    def _(j):
+        corner(2, j)
+
     for d in range(1, PLANES):
         @pl.when(from_below(d))
         def _():
@@ -395,86 +476,6 @@
         def _():
             pool_message(SIB_DOWN + d - 1, layer_at(z + d, 1 - c), sib).wait_recv()
     pool_message(SIB_OWN, layer_at(z, 1 - c), sib).wait_recv()
-
-    factor = HEAD_DIM ** (-0.5) * 1.4426950408889634
-    group = query_ref.shape[2] // HEAD_DIM
-    far_span = PLANE_BLOCKS * rows
-    near_span = span - far_span
-    contract = (((1,), (1,)), ((), ()))
-
-    def stacked_queries(h):
-        queries = query_ref[h]
-        return jnp.concatenate(
-            [queries[:, g * HEAD_DIM:(g + 1) * HEAD_DIM] for g in range(group)], axis=0
-        )
-
-    def score(query, pairs):
-        scores[:, :pairs.shape[0]] = lax.dot_general(
-            query, pairs[:, :HEAD_DIM], contract, preferred_element_type=jnp.float32
-        )
-
-    def weighted(pairs):
-        count = pairs.shape[0]
-        values = jnp.concatenate(
-            [pairs[:, HEAD_DIM:], jnp.ones((count, HEAD_DIM), jnp.bfloat16)], axis=1
-        )
-        return jnp.dot(weights[:, :count], values, preferred_element_type=jnp.float32)
-
-    def chunks():
-        for r in range(0, rows, CHUNK):
-            for g in range(group):
-                yield pl.ds(r, CHUNK), pl.ds(g * rows + r, CHUNK)
-
-    def early(h):
-        near = window[h, pl.ds(place + PLANE_BLOCKS, PLANE_BLOCKS + 1)].reshape(near_span, width)
-        pairs = jnp.concatenate([prefix[h], near], axis=0)
-        score(stacked_queries(h), pairs)
-        count = keys + near_span
-        for mask_rows, own in chunks():
-            pool_scores = scores[own, :keys] + pool_bias[h]
-            near_scores = scores[own, keys:count] + bias[mask_rows, far_span:]
-            top = factor * jnp.maximum(
-                jnp.max(pool_scores, axis=1, keepdims=True), jnp.max(near_scores, axis=1, keepdims=True)
-            )
-            weights[own, :keys] = jnp.exp2(pool_scores * factor - top).astype(jnp.bfloat16)
-            weights[own, keys:count] = jnp.exp2(near_scores * factor - top).astype(jnp.bfloat16)
-            tops[h, own] = jnp.broadcast_to(top, (CHUNK, HEAD_DIM))
-        mixed[h] = weighted(pairs)
-
-    def late(h):
-        far = window[h, pl.ds(place, PLANE_BLOCKS)].reshape(far_span, width)
-        score(stacked_queries(h), far)
-        for mask_rows, own in chunks():
-            far_scores = scores[own, :far_span] + bias[mask_rows, :far_span]
-            before = tops[h, own]
-            top = jnp.maximum(before, factor * jnp.max(far_scores, axis=1, keepdims=True))
-            weights[own, :far_span] = jnp.exp2(far_scores * factor - top[:, :1]).astype(jnp.bfloat16)
-            tops[h, own] = jnp.exp2(before - top)
-        part = weighted(far)
-        shrink = tops[h]
-        value_sum = mixed[h, :, :HEAD_DIM] * shrink + part[:, :HEAD_DIM]
-        total = mixed[h, :, HEAD_DIM:] * shrink + part[:, HEAD_DIM:]
-        result = (value_sum / total).astype(out_ref.dtype)
-        for g in range(group):
-            out_ref[h, :, g * HEAD_DIM:(g + 1) * HEAD_DIM] = result[g * rows:(g + 1) * rows]
-
-    def for_heads(j, body):
-        lax.fori_loop(0, piece, lambda i, carry: (body(j * piece + i), carry)[1], 0)
-
-    def from_sibling(k, j):
-        for kind in (KSZ, KSX, KSY, KSD):
-            arrived(kind, k, j)
-
-    @for_pieces
-    def _(j):
-        cross(2, j)
-        from_sibling(0, j)
-        from_sibling(1, j)
-        for_heads(j, early)
-
-    @for_pieces
-    def _(j):
-        corner(2, j)
 
     @for_pieces
     def _(j):

time: 58 us -> 57.3 us (0.988)
  no operation moved by 1% of the time
where the time goes in v4:
time: 57.3 us; the launch traced here: 56.4 us
  Pallas kernels  51 us (89%)
  local copies, waits for them, and re-layouts  5.23 us (9%)
    pallas_call x1, Pallas kernels, relayed(): pl.pallas_call(functools.partial(relay_kernel, page_table.shape[1]), out_...  51 us
    unnamed x9, local copies, waits for them, and re-layouts  3.51 us
    transpose x1, local copies, waits for them, and re-layouts, relayed(): return jnp.swapaxes(attended, 0, 1)  1.55 us

profile of v4, /device:TPU:17, one launch (start us, length us, event | category | flops | bytes accessed | tf_op | source)
XLA Modules:
  0.0 56.4 jit_solution(6583017015545304831)
XLA Ops:
  0.0 0.0 copy-start.1
  0.0 0.0 copy-start.2
  0.0 0.0 copy-start
  0.0 0.7 %copy-done.1 = s32[2048]{0:T(1024)S(1)} copy-done((s32[2048]{0:T(1024)S(1)}, s32[2048]{0:T(1024)}, u32[]{:S(2)}) %copy-start.1) | copy-done | bytes 8216
  0.7 0.1 dynamic_slice.3
  0.8 0.2 convert_reduce_fusion
  1.0 0.0 copy-done.2
  1.0 0.1 copy.14.start_ref
  1.1 0.0 copy-done
  1.1 1.0 %copy.20 = bf16[64,8,256]{2,0,1:T(8,128)(2,1)S(1)} copy(bf16[64,8,256]{2,1,0:T(8,128)(2,1)} %param.6) | data formatting | bytes 524288 | tf_op args[1]
  2.1 1.8 %copy.19 = bf16[64,8,1024]{2,0,1:T(8,128)(2,1)S(1)} copy(bf16[64,8,1024]{2,1,0:T(8,128)(2,1)} %param.5) | data formatting | bytes 2097152 | tf_op args[0]
  3.9 51.0 %shard_map.55 = bf16[8,64,1024]{2,1,0:T(8,128)(2,1)S(1)} custom-call(bf16[8,64,1024]{2,1,0:T(8,128)(2,1)S(1)} %bitcast.14, bf16[8,64,256]{2,1,0:T(8,128)(2,1)S(1)} %bitcast.15, s32[64,1]{1,0:T(8,128)S(1)} %copy.14.start_ref, bf16[4,16,256]{2,1,0:T(8,128)(2,1)S(1)} %bitcast.16, s32[8,128]{1,0:T(8,128)S(1)} %pad.4.table_ref), custom_call_target="tpu_custom_call" | custom-call | flops 2818572288 | bytes 2097152 | tf_op jit(solution)/shard_map/pallas_call | solution.py:531
  54.9 1.5 %copy.15 = bf16[64,8,1024]{2,1,0:T(8,128)(2,1)} copy(bf16[64,8,1024]{2,0,1:T(8,128)(2,1)S(1)} %bitcast.13) | data formatting | bytes 2097152 | tf_op jit(solution)/shard_map/transpose | solution.py:566
  (2 shorter events, 0.0 us)
Async XLA Ops:
  0.0 0.7 %copy-start.1 = (s32[2048]{0:T(1024)S(1)}, s32[2048]{0:T(1024)}, u32[]{:S(2)}) copy-start(s32[2048]{0:T(1024)} %param.7) | copy-start | bytes 24580
  0.0 1.0 %copy-start.2 = (s32[4,8]{1,0:T(4,128)S(1)}, s32[4,8]{1,0:T(4,128)}, u32[]{:S(2)}) copy-start(s32[4,8]{1,0:T(4,128)} %param.9) | copy-start | bytes 388
  0.0 1.1 %copy-start = (bf16[1,16,4,256]{3,2,1,0:T(4,128)(2,1)S(1)}, bf16[1,16,4,256]{3,2,1,0:T(4,128)(2,1)}, u32[]{:S(2)}) copy-start(bf16[1,16,4,256]{3,2,1,0:T(4,128)(2,1)} %param.8) | copy-start | bytes 98308

commit v5 on v4

--- a/solution.py
+++ b/solution.py
@@ -386,30 +386,30 @@
         )
 
     def score(query, pairs):
-        scores[:, :pairs.shape[0]] = lax.dot_general(
+        count = pairs.shape[0]
+        scores[:, :, :count] = lax.dot_general(
             query, pairs[:, :HEAD_DIM], contract, preferred_element_type=jnp.float32
-        )
+        ).reshape(group, rows, count)
 
     def weighted(pairs):
         count = pairs.shape[0]
         values = jnp.concatenate(
             [pairs[:, HEAD_DIM:], jnp.ones((count, HEAD_DIM), jnp.bfloat16)], axis=1
         )
-        return jnp.dot(weights[:, :count], values, preferred_element_type=jnp.float32)
-
-    def chunks():
-        for r in range(0, rows, CHUNK):
-            for g in range(group):
-                yield pl.ds(r, CHUNK), pl.ds(g * rows + r, CHUNK)
+        return jnp.dot(
+            weights[:, :, :count].reshape(group * rows, count), values, preferred_element_type=jnp.float32
+        )
+
+    chunks = [pl.ds(r, CHUNK) for r in range(0, rows, CHUNK)]
 
     def early(h):
         near = window[h, pl.ds(place + PLANE_BLOCKS, PLANE_BLOCKS + 1)].reshape(near_span, width)
         score(stacked_queries(h), near)
-        for mask_rows, own in chunks():
-            near_scores = scores[own, :near_span] + bias[mask_rows, far_span:]
-            top = factor * jnp.max(near_scores, axis=1, keepdims=True)
-            weights[own, :near_span] = jnp.exp2(near_scores * factor - top).astype(jnp.bfloat16)
-            tops[h, own] = jnp.broadcast_to(top, (CHUNK, HEAD_DIM))
+        for own in chunks:
+            near_scores = scores[:, own, :near_span] + bias[own, far_span:][None]
+            top = factor * jnp.max(near_scores, axis=2, keepdims=True)
+            weights[:, own, :near_span] = jnp.exp2(near_scores * factor - top).astype(jnp.bfloat16)
+            tops[h, :, own] = jnp.broadcast_to(top, (group, CHUNK, HEAD_DIM))
         mixed[h] = weighted(near)
 
     def late(h):
@@ -417,19 +417,20 @@
         far = jnp.concatenate([prefix[h], far], axis=0)
         score(stacked_queries(h), far)
         count = keys + far_span
-        for mask_rows, own in chunks():
-            pool_scores = scores[own, :keys] + pool_bias[h]
-            far_scores = scores[own, keys:count] + bias[mask_rows, :far_span]
-            before = tops[h, own]
+        pool_mask = pool_bias[h][None]
+        for own in chunks:
+            pool_scores = scores[:, own, :keys] + pool_mask
+            far_scores = scores[:, own, keys:count] + bias[own, :far_span][None]
+            before = tops[h, :, own]
             top = jnp.maximum(
-                jnp.max(pool_scores, axis=1, keepdims=True), jnp.max(far_scores, axis=1, keepdims=True)
+                jnp.max(pool_scores, axis=2, keepdims=True), jnp.max(far_scores, axis=2, keepdims=True)
             )
             top = jnp.maximum(before, factor * top)
-            weights[own, :keys] = jnp.exp2(pool_scores * factor - top[:, :1]).astype(jnp.bfloat16)
-            weights[own, keys:count] = jnp.exp2(far_scores * factor - top[:, :1]).astype(jnp.bfloat16)
-            tops[h, own] = jnp.exp2(before - top)
+            weights[:, own, :keys] = jnp.exp2(pool_scores * factor - top[..., :1]).astype(jnp.bfloat16)
+            weights[:, own, keys:count] = jnp.exp2(far_scores * factor - top[..., :1]).astype(jnp.bfloat16)
+            tops[h, :, own] = jnp.exp2(before - top)
         part = weighted(far)
-        shrink = tops[h]
+        shrink = tops[h].reshape(group * rows, HEAD_DIM)
         value_sum = mixed[h, :, :HEAD_DIM] * shrink + part[:, :HEAD_DIM]
         total = mixed[h, :, HEAD_DIM:] * shrink + part[:, HEAD_DIM:]
         result = (value_sum / total).astype(out_ref.dtype)
@@ -539,10 +540,10 @@
             pltpu.VMEM((2, 8, 128), jnp.int32),
             pltpu.VMEM((rows, span), jnp.float32),
             pltpu.VMEM((heads, 1, pool_keys), jnp.float32),
-            pltpu.VMEM((rows * (wide // HEAD_DIM), pool_keys + (PLANE_BLOCKS + 1) * rows), jnp.float32),
-            pltpu.VMEM((rows * (wide // HEAD_DIM), pool_keys + (PLANE_BLOCKS + 1) * rows), jnp.bfloat16),
+            pltpu.VMEM((wide // HEAD_DIM, rows, pool_keys + PLANE_BLOCKS * rows), jnp.float32),
+            pltpu.VMEM((wide // HEAD_DIM, rows, pool_keys + PLANE_BLOCKS * rows), jnp.bfloat16),
             pltpu.VMEM((heads, rows * (wide // HEAD_DIM), 2 * HEAD_DIM), jnp.float32),
-            pltpu.VMEM((heads, rows * (wide // HEAD_DIM), HEAD_DIM), jnp.float32),
+            pltpu.VMEM((heads, wide // HEAD_DIM, rows, HEAD_DIM), jnp.float32),
             pltpu.SemaphoreType.DMA((8, 3, PIECES)),
             pltpu.SemaphoreType.DMA((8, 3, PIECES)),
             pltpu.SemaphoreType.DMA((16,)),

time: 57.3 us -> 56.5 us (0.986)
  Pallas kernels: 51 us -> 50.1 us
    pallas_call x1, Pallas kernels: 51 us -> 50.1 us  [relayed(): pl.pallas_call(functools.partial(relay_kernel, page_table.shape[1]), out_...]
where the time goes in v5:
time: 56.5 us; the launch traced here: 55.6 us
  Pallas kernels  50.1 us (89%)
  local copies, waits for them, and re-layouts  5.23 us (9%)
    pallas_call x1, Pallas kernels, relayed(): pl.pallas_call(functools.partial(relay_kernel, page_table.shape[1]), out_...  50.1 us
    unnamed x9, local copies, waits for them, and re-layouts  3.51 us
    transpose x1, local copies, waits for them, and re-layouts, relayed(): return jnp.swapaxes(attended, 0, 1)  1.55 us

profile of v5, /device:TPU:17, one launch (start us, length us, event | category | flops | bytes accessed | tf_op | source)
XLA Modules:
  0.0 55.6 jit_solution(11945716944262322739)
XLA Ops:
  0.0 0.0 copy-start.1
  0.0 0.0 copy-start.2
  0.0 0.0 copy-start
  0.0 0.7 %copy-done.1 = s32[2048]{0:T(1024)S(1)} copy-done((s32[2048]{0:T(1024)S(1)}, s32[2048]{0:T(1024)}, u32[]{:S(2)}) %copy-start.1) | copy-done | bytes 8216
  0.7 0.1 dynamic_slice.3
  0.8 0.2 convert_reduce_fusion
  1.0 0.0 copy-done.2
  1.0 0.1 copy.14.start_ref
  1.1 0.0 copy-done
  1.1 1.0 %copy.20 = bf16[64,8,256]{2,0,1:T(8,128)(2,1)S(1)} copy(bf16[64,8,256]{2,1,0:T(8,128)(2,1)} %param.6) | data formatting | bytes 524288 | tf_op args[1]
  2.1 1.8 %copy.19 = bf16[64,8,1024]{2,0,1:T(8,128)(2,1)S(1)} copy(bf16[64,8,1024]{2,1,0:T(8,128)(2,1)} %param.5) | data formatting | bytes 2097152 | tf_op args[0]
  3.9 50.1 %shard_map.55 = bf16[8,64,1024]{2,1,0:T(8,128)(2,1)S(1)} custom-call(bf16[8,64,1024]{2,1,0:T(8,128)(2,1)S(1)} %bitcast.14, bf16[8,64,256]{2,1,0:T(8,128)(2,1)S(1)} %bitcast.15, s32[64,1]{1,0:T(8,128)S(1)} %copy.14.start_ref, bf16[4,16,256]{2,1,0:T(8,128)(2,1)S(1)} %bitcast.16, s32[8,128]{1,0:T(8,128)S(1)} %pad.4.table_ref), custom_call_target="tpu_custom_call" | custom-call | flops 2818572288 | bytes 2097152 | tf_op jit(solution)/shard_map/pallas_call | solution.py:532
  54.1 1.5 %copy.15 = bf16[64,8,1024]{2,1,0:T(8,128)(2,1)} copy(bf16[64,8,1024]{2,0,1:T(8,128)(2,1)S(1)} %bitcast.13) | data formatting | bytes 2097152 | tf_op jit(solution)/shard_map/transpose | solution.py:567
  (2 shorter events, 0.0 us)
Async XLA Ops:
  0.0 0.7 %copy-start.1 = (s32[2048]{0:T(1024)S(1)}, s32[2048]{0:T(1024)}, u32[]{:S(2)}) copy-start(s32[2048]{0:T(1024)} %param.7) | copy-start | bytes 24580
  0.0 1.0 %copy-start.2 = (s32[4,8]{1,0:T(4,128)S(1)}, s32[4,8]{1,0:T(4,128)}, u32[]{:S(2)}) copy-start(s32[4,8]{1,0:T(4,128)} %param.9) | copy-start | bytes 388
  0.0 1.1 %copy-start = (bf16[1,16,4,256]{3,2,1,0:T(4,128)(2,1)S(1)}, bf16[1,16,4,256]{3,2,1,0:T(4,128)(2,1)}, u32[]{:S(2)}) copy-start(bf16[1,16,4,256]{3,2,1,0:T(4,128)(2,1)} %param.8) | copy-start | bytes 98308

commit v6 on v5

--- a/solution.py
+++ b/solution.py
@@ -106,7 +106,7 @@
 def relay_kernel(
     listed,
     query_ref, pairs_ref, start_ref, pool_ref, table_ref, out_ref,
-    window, prefix, tables, bias, pool_bias, scores, weights, mixed, tops,
+    window, prefix, tables, bias, pool_bias, scores, weights, mixed, tops, shrinks,
     send_sem, recv_sem, pool_send, pool_recv,
 ):
     heads, rows, width = pairs_ref.shape
@@ -173,8 +173,8 @@
     }
     targets = {KZ: up, KX: xn, KY: yn, KSZ: sib, KSX: sib, KSY: sib, KSD: sib}
 
-    def x_first(j):
-        return j < PIECES // 2
+    def x_half(j):
+        return j // (PIECES // 2)
 
     def outgoing(kind, k, j):
         return message(kind, k, j, k - 1 if kind == KZ else k, *source[kind], targets[kind])
@@ -211,12 +211,13 @@
         return present(k)
 
     def corner_sends(k, j, by_y):
-        return takes_x(k) & x_first(j) if by_y else gives_x(k) & jnp.logical_not(x_first(j))
+        return takes_x(k) & (x_half(j) == 0) if by_y else gives_x(k) & (x_half(j) == 1)
 
     started = []
 
     def start(kind, k, j):
-        started.append((kind, k))
+        if (kind, k) not in started:
+            started.append((kind, k))
 
         @pl.when(sends(kind, k))
         def _():
@@ -307,10 +308,6 @@
 
     plane_rows = PLANE_BLOCKS * rows
 
-    @pl.when(z < 2)
-    def _():
-        window[:, :PLANE_BLOCKS] = jnp.zeros((heads, PLANE_BLOCKS, rows, width), window.dtype)
-
     @pl.when(z < 1)
     def _():
         window[:, PLANE_BLOCKS:2 * PLANE_BLOCKS] = jnp.zeros((heads, PLANE_BLOCKS, rows, width), window.dtype)
@@ -318,8 +315,8 @@
     span = bias.shape[1]
     column = lax.broadcasted_iota(jnp.int32, (rows, span), 1)
     row = lax.broadcasted_iota(jnp.int32, (rows, span), 0)
-    base = (z * PLANE_BLOCKS + place) * rows - 2 * plane_rows
-    seen = (column >= start_ref[...] - base) & (column <= row + 2 * plane_rows)
+    base = z * plane_rows - 2 * plane_rows
+    seen = (column >= start_ref[...] - base) & (column <= row + place * rows + 2 * plane_rows)
     bias[...] = jnp.where(seen, 0.0, -1e30)
 
     py_in.wait_recv()
@@ -351,108 +348,9 @@
     def _(j):
         cross(0, j)
 
-    pool_arrived(1)
-
-    @for_pieces
-    def _(j):
-        arrived(KZ, 2, j)
-        for kind, k in ((KX, 2), (KY, 2), (KSZ, 2)):
-            start(kind, k, j)
-
-    @for_pieces
-    def _(j):
-        cross(1, j)
-        corner(0, j)
-
-    pool_arrived(2)
-
-    @for_pieces
-    def _(j):
-        corner(1, j)
-
-    pool_arrived(3)
-
-    factor = HEAD_DIM ** (-0.5) * 1.4426950408889634
-    group = query_ref.shape[2] // HEAD_DIM
-    keys = PLANES * 4 * page_rows
-    far_span = PLANE_BLOCKS * rows
-    near_span = span - far_span
-    contract = (((1,), (1,)), ((), ()))
-
-    def stacked_queries(h):
-        queries = query_ref[h]
-        return jnp.concatenate(
-            [queries[:, g * HEAD_DIM:(g + 1) * HEAD_DIM] for g in range(group)], axis=0
-        )
-
-    def score(query, pairs):
-        count = pairs.shape[0]
-        scores[:, :, :count] = lax.dot_general(
-            query, pairs[:, :HEAD_DIM], contract, preferred_element_type=jnp.float32
-        ).reshape(group, rows, count)
-
-    def weighted(pairs):
-        count = pairs.shape[0]
-        values = jnp.concatenate(
-            [pairs[:, HEAD_DIM:], jnp.ones((count, HEAD_DIM), jnp.bfloat16)], axis=1
-        )
-        return jnp.dot(
-            weights[:, :, :count].reshape(group * rows, count), values, preferred_element_type=jnp.float32
-        )
-
-    chunks = [pl.ds(r, CHUNK) for r in range(0, rows, CHUNK)]
-
-    def early(h):
-        near = window[h, pl.ds(place + PLANE_BLOCKS, PLANE_BLOCKS + 1)].reshape(near_span, width)
-        score(stacked_queries(h), near)
-        for own in chunks:
-            near_scores = scores[:, own, :near_span] + bias[own, far_span:][None]
-            top = factor * jnp.max(near_scores, axis=2, keepdims=True)
-            weights[:, own, :near_span] = jnp.exp2(near_scores * factor - top).astype(jnp.bfloat16)
-            tops[h, :, own] = jnp.broadcast_to(top, (group, CHUNK, HEAD_DIM))
-        mixed[h] = weighted(near)
-
-    def late(h):
-        far = window[h, pl.ds(place, PLANE_BLOCKS)].reshape(far_span, width)
-        far = jnp.concatenate([prefix[h], far], axis=0)
-        score(stacked_queries(h), far)
-        count = keys + far_span
-        pool_mask = pool_bias[h][None]
-        for own in chunks:
-            pool_scores = scores[:, own, :keys] + pool_mask
-            far_scores = scores[:, own, keys:count] + bias[own, :far_span][None]
-            before = tops[h, :, own]
-            top = jnp.maximum(
-                jnp.max(pool_scores, axis=2, keepdims=True), jnp.max(far_scores, axis=2, keepdims=True)
-            )
-            top = jnp.maximum(before, factor * top)
-            weights[:, own, :keys] = jnp.exp2(pool_scores * factor - top[..., :1]).astype(jnp.bfloat16)
-            weights[:, own, keys:count] = jnp.exp2(far_scores * factor - top[..., :1]).astype(jnp.bfloat16)
-            tops[h, :, own] = jnp.exp2(before - top)
-        part = weighted(far)
-        shrink = tops[h].reshape(group * rows, HEAD_DIM)
-        value_sum = mixed[h, :, :HEAD_DIM] * shrink + part[:, :HEAD_DIM]
-        total = mixed[h, :, HEAD_DIM:] * shrink + part[:, HEAD_DIM:]
-        result = (value_sum / total).astype(out_ref.dtype)
-        for g in range(group):
-            out_ref[h, :, g * HEAD_DIM:(g + 1) * HEAD_DIM] = result[g * rows:(g + 1) * rows]
-
-    def for_heads(j, body):
-        lax.fori_loop(0, piece, lambda i, carry: (body(j * piece + i), carry)[1], 0)
-
-    def from_sibling(k, j):
-        for kind in (KSZ, KSX, KSY, KSD):
-            arrived(kind, k, j)
-
-    @for_pieces
-    def _(j):
-        cross(2, j)
-        from_sibling(0, j)
-        from_sibling(1, j)
-        for_heads(j, early)
-
     table_in.wait_recv()
     pages = PLANES * 4
+    keys = pages * page_rows
     slot = lax.broadcasted_iota(jnp.int32, (8, keys), 1) // page_rows
     page = (slot % (pages // 2)) * 2 + slot // (pages // 2)
     for side in range(2):
@@ -464,10 +362,138 @@
         for i in range(half):
             pool_bias[side * half + i] = mask[i:i + 1]
 
+    factor = HEAD_DIM ** (-0.5) * 1.4426950408889634
+    group = query_ref.shape[2] // HEAD_DIM
+    contract = (((1,), (1,)), ((), ()))
+
+    def stacked_queries(h):
+        queries = query_ref[h]
+        return jnp.concatenate(
+            [queries[:, g * HEAD_DIM:(g + 1) * HEAD_DIM] for g in range(group)], axis=0
+        )
+
+    def score(query, pairs):
+        count = pairs.shape[0]
+        scores[:, :, :count] = lax.dot_general(
+            query, pairs[:, :HEAD_DIM], contract, preferred_element_type=jnp.float32
+        ).reshape(group, rows, count)
+
+    def weighted(pairs):
+        count = pairs.shape[0]
+        values = jnp.concatenate(
+            [pairs[:, HEAD_DIM:], jnp.ones((count, HEAD_DIM), jnp.bfloat16)], axis=1
+        )
+        return jnp.dot(
+            weights[:, :, :count].reshape(group * rows, count), values, preferred_element_type=jnp.float32
+        )
+
+    chunks = [pl.ds(r, CHUNK) for r in range(0, rows, CHUNK)]
+
+    def attend(h, first_slot, slots, with_pool, begins):
+        pairs = window[h, first_slot:first_slot + slots].reshape(slots * rows, width)
+        columns = slice(first_slot * rows, (first_slot + slots) * rows)
+        at = keys if with_pool else 0
+        if with_pool:
+            pairs = jnp.concatenate([prefix[h], pairs], axis=0)
+        score(stacked_queries(h), pairs)
+        count = pairs.shape[0]
+        for own in chunks:
+            near_scores = scores[:, own, at:count] + bias[own, columns][None]
+            top = jnp.max(near_scores, axis=2, keepdims=True)
+            if with_pool:
+                pool_scores = scores[:, own, :at] + pool_bias[h][None]
+                top = jnp.maximum(top, jnp.max(pool_scores, axis=2, keepdims=True))
+            top = jnp.broadcast_to(factor * top, (group, CHUNK, HEAD_DIM))
+            if not begins:
+                before = tops[h, :, own]
+                top = jnp.maximum(before, top)
+                shrinks[:, own] = jnp.exp2(before - top)
+            tops[h, :, own] = top
+            if with_pool:
+                weights[:, own, :at] = jnp.exp2(pool_scores * factor - top[..., :1]).astype(jnp.bfloat16)
+            weights[:, own, at:count] = jnp.exp2(near_scores * factor - top[..., :1]).astype(jnp.bfloat16)
+        part = weighted(pairs)
+        if begins:
+            mixed[h] = part
+        else:
+            shrink = shrinks[...].reshape(group * rows, HEAD_DIM)
+            mixed[h, :, :HEAD_DIM] = mixed[h, :, :HEAD_DIM] * shrink + part[:, :HEAD_DIM]
+            mixed[h, :, HEAD_DIM:] = mixed[h, :, HEAD_DIM:] * shrink + part[:, HEAD_DIM:]
+
+    def finish(h):
+        result = (mixed[h, :, :HEAD_DIM] / mixed[h, :, HEAD_DIM:]).astype(out_ref.dtype)
+        for g in range(group):
+            out_ref[h, :, g * HEAD_DIM:(g + 1) * HEAD_DIM] = result[g * rows:(g + 1) * rows]
+
+    half_plane = PLANE_BLOCKS // 2
+
+    def own_part(h):
+        @pl.when(x == 0)
+        def _():
+            attend(h, 2 * PLANE_BLOCKS, half_plane, False, True)
+
+        @pl.when(x == 1)
+        def _():
+            attend(h, 2 * PLANE_BLOCKS, PLANE_BLOCKS, False, True)
+
+    def next_part(h):
+        attend(h, PLANE_BLOCKS, PLANE_BLOCKS, True, False)
+
+    def last_part(h):
+        @pl.when((z >= 2) & (x == 0))
+        def _():
+            attend(h, 0, PLANE_BLOCKS, False, False)
+
+        @pl.when((z >= 2) & (x == 1))
+        def _():
+            attend(h, half_plane, half_plane, False, False)
+
+        finish(h)
+
+    def for_heads(body):
+        lax.fori_loop(0, heads, lambda h, carry: (body(h), carry)[1], 0)
+
+    def from_sibling(k):
+        @for_pieces
+        def _(j):
+            for kind in (KSZ, KSX, KSY, KSD):
+                arrived(kind, k, j)
+
     @for_pieces
     def _(j):
-        corner(2, j)
-
+        corner(0, j)
+
+    from_sibling(0)
+
+    @for_heads
+    def _(h):
+        own_part(h)
+
+        @pl.when(h == 1)
+        def _():
+            @for_pieces
+            def _(j):
+                arrived(KZ, 2, j)
+                for kind, k in ((KX, 2), (KY, 2), (KSZ, 2)):
+                    start(kind, k, j)
+
+            pool_arrived(1)
+
+        @pl.when(h == 3)
+        def _():
+            cross(1, 0)
+
+        @pl.when(h == 5)
+        def _():
+            for j in range(1, PIECES):
+                cross(1, j)
+            pool_arrived(2)
+
+    @for_pieces
+    def _(j):
+        corner(1, j)
+
+    pool_arrived(3)
     for d in range(1, PLANES):
         @pl.when(from_below(d))
         def _():
@@ -478,10 +504,30 @@
             pool_message(SIB_DOWN + d - 1, layer_at(z + d, 1 - c), sib).wait_recv()
     pool_message(SIB_OWN, layer_at(z, 1 - c), sib).wait_recv()
 
-    @for_pieces
-    def _(j):
-        from_sibling(2, j)
-        for_heads(j, late)
+    from_sibling(1)
+
+    @for_heads
+    def _(h):
+        next_part(h)
+
+        @pl.when(h == 1)
+        def _():
+            cross(2, 0)
+
+        @pl.when(h == 3)
+        def _():
+            for j in range(1, PIECES):
+                cross(2, j)
+
+        @pl.when(h == 5)
+        def _():
+            @for_pieces
+            def _(j):
+                corner(2, j)
+
+    from_sibling(2)
+
+    for_heads(last_part)
 
     @for_pieces
     def _(j):
@@ -526,7 +572,7 @@
     own_ids = lax.dynamic_slice_in_dim(branch_ids, block * rows, rows, 0)
     starts = jnp.sum((branch_ids[None, :] < own_ids[:, None]).astype(jnp.int32), axis=1, keepdims=True)
     table = jnp.pad(page_table, ((0, 8 - page_table.shape[0]), (0, 128 - page_table.shape[1])))
-    span = 2 * PLANE_BLOCKS * rows + rows
+    span = 3 * PLANE_BLOCKS * rows
     pool_keys = PLANES * 4 * page_rows
     vmem = pl.BlockSpec(memory_space=pltpu.VMEM)
     attended = pl.pallas_call(
@@ -544,6 +590,7 @@
             pltpu.VMEM((wide // HEAD_DIM, rows, pool_keys + PLANE_BLOCKS * rows), jnp.bfloat16),
             pltpu.VMEM((heads, rows * (wide // HEAD_DIM), 2 * HEAD_DIM), jnp.float32),
             pltpu.VMEM((heads, wide // HEAD_DIM, rows, HEAD_DIM), jnp.float32),
+            pltpu.VMEM((wide // HEAD_DIM, rows, HEAD_DIM), jnp.float32),
             pltpu.SemaphoreType.DMA((8, 3, PIECES)),
             pltpu.SemaphoreType.DMA((8, 3, PIECES)),
             pltpu.SemaphoreType.DMA((16,)),

time: 56.5 us -> 61.8 us (1.094)
  Pallas kernels: 50.1 us -> 55.8 us
    pallas_call x1, Pallas kernels: 50.1 us -> 55.8 us  [relayed(): pl.pallas_call(functools.partial(relay_kernel, page_table.shape[1]), out_...]
where the time goes in v6:
time: 61.8 us; the launch traced here: 61.3 us
  Pallas kernels  55.8 us (90%)
  local copies, waits for them, and re-layouts  5.23 us (8%)
    pallas_call x1, Pallas kernels, relayed(): pl.pallas_call(functools.partial(relay_kernel, page_table.shape[1]), out_...  55.8 us
    unnamed x9, local copies, waits for them, and re-layouts  3.51 us
    transpose x1, local copies, waits for them, and re-layouts, relayed(): return jnp.swapaxes(attended, 0, 1)  1.55 us

profile of v6, /device:TPU:17, one launch (start us, length us, event | category | flops | bytes accessed | tf_op | source)
XLA Modules:
  0.0 61.3 jit_solution(16966170263303191247)
XLA Ops:
  0.0 0.0 copy-start.1
  0.0 0.0 copy-start.2
  0.0 0.0 copy-start
  0.0 0.7 %copy-done.1 = s32[2048]{0:T(1024)S(1)} copy-done((s32[2048]{0:T(1024)S(1)}, s32[2048]{0:T(1024)}, u32[]{:S(2)}) %copy-start.1) | copy-done | bytes 8216
  0.7 0.1 dynamic_slice.3
  0.8 0.2 convert_reduce_fusion
  1.0 0.0 copy-done.2
  1.0 0.1 copy.14.start_ref
  1.1 0.0 copy-done
  1.1 1.0 %copy.20 = bf16[64,8,256]{2,0,1:T(8,128)(2,1)S(1)} copy(bf16[64,8,256]{2,1,0:T(8,128)(2,1)} %param.6) | data formatting | bytes 524288 | tf_op args[1]
  2.1 1.8 %copy.19 = bf16[64,8,1024]{2,0,1:T(8,128)(2,1)S(1)} copy(bf16[64,8,1024]{2,1,0:T(8,128)(2,1)} %param.5) | data formatting | bytes 2097152 | tf_op args[0]
  3.9 55.8 %shard_map.55 = bf16[8,64,1024]{2,1,0:T(8,128)(2,1)S(1)} custom-call(bf16[8,64,1024]{2,1,0:T(8,128)(2,1)S(1)} %bitcast.14, bf16[8,64,256]{2,1,0:T(8,128)(2,1)S(1)} %bitcast.15, s32[64,1]{1,0:T(8,128)S(1)} %copy.14.start_ref, bf16[4,16,256]{2,1,0:T(8,128)(2,1)S(1)} %bitcast.16, s32[8,128]{1,0:T(8,128)S(1)} %pad.4.table_ref), custom_call_target="tpu_custom_call" | custom-call | flops 3758096384 | bytes 2097152 | tf_op jit(solution)/shard_map/pallas_call | solution.py:578
  59.7 1.5 %copy.15 = bf16[64,8,1024]{2,1,0:T(8,128)(2,1)} copy(bf16[64,8,1024]{2,0,1:T(8,128)(2,1)S(1)} %bitcast.13) | data formatting | bytes 2097152 | tf_op jit(solution)/shard_map/transpose | solution.py:614
  (2 shorter events, 0.0 us)
Async XLA Ops:
  0.0 0.7 %copy-start.1 = (s32[2048]{0:T(1024)S(1)}, s32[2048]{0:T(1024)}, u32[]{:S(2)}) copy-start(s32[2048]{0:T(1024)} %param.7) | copy-start | bytes 24580
  0.0 1.0 %copy-start.2 = (s32[4,8]{1,0:T(4,128)S(1)}, s32[4,8]{1,0:T(4,128)}, u32[]{:S(2)}) copy-start(s32[4,8]{1,0:T(4,128)} %param.9) | copy-start | bytes 388
  0.0 1.1 %copy-start = (bf16[1,16,4,256]{3,2,1,0:T(4,128)(2,1)S(1)}, bf16[1,16,4,256]{3,2,1,0:T(4,128)(2,1)}, u32[]{:S(2)}) copy-start(bf16[1,16,4,256]{3,2,1,0:T(4,128)(2,1)} %param.8) | copy-start | bytes 98308

commit v7 on v1

--- a/solution.py
+++ b/solution.py
@@ -98,6 +98,7 @@
 
 PLANES = 4
 PLANE_BLOCKS = 8
+CHUNK = 16
 PIECES = 4
 KZ, KX, KY, KD, KSZ, KSX, KSY, KSD = range(8)
 
@@ -105,7 +106,7 @@
 def relay_kernel(
     listed,
     query_ref, pairs_ref, start_ref, pool_ref, table_ref, out_ref,
-    window, prefix, tables, bias, pool_bias,
+    window, prefix, tables, bias, pool_bias, scores, weights,
     send_sem, recv_sem, pool_send, pool_recv,
 ):
     heads, rows, width = pairs_ref.shape
@@ -408,45 +409,57 @@
 
     factor = HEAD_DIM ** (-0.5) * 1.4426950408889634
     group = query_ref.shape[2] // HEAD_DIM
-    ones = jnp.ones((span, HEAD_DIM), jnp.bfloat16)
-    pool_ones = jnp.ones((keys, HEAD_DIM), jnp.bfloat16)
     contract = (((1,), (1,)), ((), ()))
-
-    def one_head(h, carry):
+    count = keys + span
+
+    def pairs_of(h):
+        near = window[h, pl.ds(place, 2 * PLANE_BLOCKS + 1)].reshape(span, width)
+        return jnp.concatenate([prefix[h], near], axis=0)
+
+    def score(h, lane):
         queries = query_ref[h]
         query = jnp.concatenate(
             [queries[:, g * HEAD_DIM:(g + 1) * HEAD_DIM] for g in range(group)], axis=0
         )
-        near = window[h, pl.ds(place, 2 * PLANE_BLOCKS + 1)].reshape(span, width)
-        far = prefix[h]
-        near_scores = lax.dot_general(
-            query, near[:, :HEAD_DIM], contract, preferred_element_type=jnp.float32
+        scores[lane] = lax.dot_general(
+            query, pairs_of(h)[:, :HEAD_DIM], contract, preferred_element_type=jnp.float32
         )
-        near_scores = (near_scores.reshape(group, rows, span) + bias[...][None]).reshape(group * rows, span)
-        far_scores = lax.dot_general(
-            query, far[:, :HEAD_DIM], contract, preferred_element_type=jnp.float32
+
+    def soften(h, lane):
+        for r in range(0, rows, CHUNK):
+            mask = bias[r:r + CHUNK, :]
+            for g in range(group):
+                own = slice(g * rows + r, g * rows + r + CHUNK)
+                pool_scores = scores[lane, own, :keys] + pool_bias[h]
+                near_scores = scores[lane, own, keys:] + mask
+                top = factor * jnp.maximum(
+                    jnp.max(pool_scores, axis=1, keepdims=True), jnp.max(near_scores, axis=1, keepdims=True)
+                )
+                weights[lane, own, :keys] = jnp.exp2(pool_scores * factor - top).astype(jnp.bfloat16)
+                weights[lane, own, keys:] = jnp.exp2(near_scores * factor - top).astype(jnp.bfloat16)
+
+    def mix(h, lane):
+        values = jnp.concatenate(
+            [pairs_of(h)[:, HEAD_DIM:], jnp.ones((count, HEAD_DIM), jnp.bfloat16)], axis=1
         )
-        far_scores = far_scores + pool_bias[h]
-        top = jnp.maximum(
-            jnp.max(near_scores, axis=1, keepdims=True), jnp.max(far_scores, axis=1, keepdims=True)
-        )
-        near_weights = jnp.exp2((near_scores - top) * factor).astype(jnp.bfloat16)
-        far_weights = jnp.exp2((far_scores - top) * factor).astype(jnp.bfloat16)
-        mixed = jnp.dot(
-            near_weights,
-            jnp.concatenate([near[:, HEAD_DIM:], ones], axis=1),
-            preferred_element_type=jnp.float32,
-        ) + jnp.dot(
-            far_weights,
-            jnp.concatenate([far[:, HEAD_DIM:], pool_ones], axis=1),
-            preferred_element_type=jnp.float32,
-        )
+        mixed = jnp.dot(weights[lane], values, preferred_element_type=jnp.float32)
         result = (mixed[:, :HEAD_DIM] / mixed[:, HEAD_DIM:]).astype(out_ref.dtype)
         for g in range(group):
             out_ref[h, :, g * HEAD_DIM:(g + 1) * HEAD_DIM] = result[g * rows:(g + 1) * rows]
+
+    score(0, 0)
+
+    def two_heads(i, carry):
+        h = 2 * i
+        score(h + 1, 1)
+        soften(h, 0)
+        mix(h, 0)
+        score(jnp.minimum(h + 2, heads - 1), 0)
+        soften(h + 1, 1)
+        mix(h + 1, 1)
         return carry
 
-    lax.fori_loop(0, heads, one_head, 0)
+    lax.fori_loop(0, heads // 2, two_heads, 0)
 
     @for_pieces
     def _(j):
@@ -505,6 +518,8 @@
             pltpu.VMEM((2, 8, 128), jnp.int32),
             pltpu.VMEM((rows, span), jnp.float32),
             pltpu.VMEM((heads, 1, pool_keys), jnp.float32),
+            pltpu.VMEM((2, rows * (wide // HEAD_DIM), pool_keys + span), jnp.float32),
+            pltpu.VMEM((2, rows * (wide // HEAD_DIM), pool_keys + span), jnp.bfloat16),
             pltpu.SemaphoreType.DMA((8, 3, PIECES)),
             pltpu.SemaphoreType.DMA((8, 3, PIECES)),
             pltpu.SemaphoreType.DMA((16,)),

time: 54.9 us -> 50.4 us (0.918)
  Pallas kernels: 49.1 us -> 44.7 us
    pallas_call x1, Pallas kernels: 49.1 us -> 44.7 us  [relayed(): pl.pallas_call(functools.partial(relay_kernel, page_table.shape[1]), out_...]
where the time goes in v7:
time: 50.4 us; the launch traced here: 50.2 us
  Pallas kernels  44.7 us (89%)
  local copies, waits for them, and re-layouts  5.23 us (10%)
    pallas_call x1, Pallas kernels, relayed(): pl.pallas_call(functools.partial(relay_kernel, page_table.shape[1]), out_...  44.7 us
    unnamed x9, local copies, waits for them, and re-layouts  3.51 us
    transpose x1, local copies, waits for them, and re-layouts, relayed(): return jnp.swapaxes(attended, 0, 1)  1.55 us

profile of v7, /device:TPU:17, one launch (start us, length us, event | category | flops | bytes accessed | tf_op | source)
XLA Modules:
  0.0 50.2 jit_solution(4118459789853513484)
XLA Ops:
  0.0 0.0 copy-start.1
  0.0 0.0 copy-start.2
  0.0 0.0 copy-start
  0.0 0.7 %copy-done.1 = s32[2048]{0:T(1024)S(1)} copy-done((s32[2048]{0:T(1024)S(1)}, s32[2048]{0:T(1024)}, u32[]{:S(2)}) %copy-start.1) | copy-done | bytes 8216
  0.7 0.1 dynamic_slice.3
  0.8 0.2 convert_reduce_fusion
  1.0 0.0 copy-done.2
  1.0 0.1 copy.14.start_ref
  1.1 0.0 copy-done
  1.1 1.0 %copy.20 = bf16[64,8,256]{2,0,1:T(8,128)(2,1)S(1)} copy(bf16[64,8,256]{2,1,0:T(8,128)(2,1)} %param.6) | data formatting | bytes 524288 | tf_op args[1]
  2.1 1.8 %copy.19 = bf16[64,8,1024]{2,0,1:T(8,128)(2,1)S(1)} copy(bf16[64,8,1024]{2,1,0:T(8,128)(2,1)} %param.5) | data formatting | bytes 2097152 | tf_op args[0]
  3.9 44.7 %shard_map.55 = bf16[8,64,1024]{2,1,0:T(8,128)(2,1)S(1)} custom-call(bf16[8,64,1024]{2,1,0:T(8,128)(2,1)S(1)} %bitcast.14, bf16[8,64,256]{2,1,0:T(8,128)(2,1)S(1)} %bitcast.15, s32[64,1]{1,0:T(8,128)S(1)} %copy.14.start_ref, bf16[4,16,256]{2,1,0:T(8,128)(2,1)S(1)} %bitcast.16, s32[8,128]{1,0:T(8,128)S(1)} %pad.4.table_ref), custom_call_target="tpu_custom_call" | custom-call | flops 2818572288 | bytes 2097152 | tf_op jit(solution)/shard_map/pallas_call | solution.py:510
  48.6 1.5 %copy.15 = bf16[64,8,1024]{2,1,0:T(8,128)(2,1)} copy(bf16[64,8,1024]{2,0,1:T(8,128)(2,1)S(1)} %bitcast.13) | data formatting | bytes 2097152 | tf_op jit(solution)/shard_map/transpose | solution.py:543
  (2 shorter events, 0.0 us)
Async XLA Ops:
  0.0 0.7 %copy-start.1 = (s32[2048]{0:T(1024)S(1)}, s32[2048]{0:T(1024)}, u32[]{:S(2)}) copy-start(s32[2048]{0:T(1024)} %param.7) | copy-start | bytes 24580
  0.0 1.0 %copy-start.2 = (s32[4,8]{1,0:T(4,128)S(1)}, s32[4,8]{1,0:T(4,128)}, u32[]{:S(2)}) copy-start(s32[4,8]{1,0:T(4,128)} %param.9) | copy-start | bytes 388
  0.0 1.1 %copy-start = (bf16[1,16,4,256]{3,2,1,0:T(4,128)(2,1)S(1)}, bf16[1,16,4,256]{3,2,1,0:T(4,128)(2,1)}, u32[]{:S(2)}) copy-start(bf16[1,16,4,256]{3,2,1,0:T(4,128)(2,1)} %param.8) | copy-start | bytes 98308

commit v8 on v7

--- a/solution.py
+++ b/solution.py
@@ -211,6 +211,8 @@
         return present(k)
 
     def corner_sends(k, j, by_y):
+        if k != 1:
+            return gives_x(k)
         return takes_x(k) & x_first(j) if by_y else gives_x(k) & jnp.logical_not(x_first(j))
 
     started = []
@@ -336,12 +338,16 @@
     pool_message(SIB_OWN, layer_at(z, c), sib).start()
 
     def cross(k, j):
-        arrived(KX, k, j)
-        corner_start(k, j, True)
-        start(KSX, k, j)
+        if k == 1:
+            arrived(KX, k, j)
+            corner_start(k, j, True)
+            start(KSX, k, j)
         arrived(KY, k, j)
         corner_start(k, j, False)
         start(KSY, k, j)
+        if k != 1:
+            arrived(KX, k, j)
+            start(KSX, k, j)
 
     def corner(k, j):
         arrived(KD, k, j)
@@ -469,7 +475,7 @@
                 outgoing(kind, k, j).wait_send()
 
         for k in range(3):
-            for by_y in (True, False):
+            for by_y in (True, False) if k == 1 else (False,):
                 @pl.when(corner_sends(k, j, by_y))
                 def _():
                     corner_out(k, j, by_y).wait_send()

time: 50.4 us -> 48.4 us (0.960)
  Pallas kernels: 44.7 us -> 42.6 us
    pallas_call x1, Pallas kernels: 44.7 us -> 42.6 us  [relayed(): pl.pallas_call(functools.partial(relay_kernel, page_table.shape[1]), out_...]
where the time goes in v8:
time: 48.4 us; the launch traced here: 48.1 us
  Pallas kernels  42.6 us (88%)
  local copies, waits for them, and re-layouts  5.23 us (11%)
    pallas_call x1, Pallas kernels, relayed(): pl.pallas_call(functools.partial(relay_kernel, page_table.shape[1]), out_...  42.6 us
    unnamed x9, local copies, waits for them, and re-layouts  3.51 us
    transpose x1, local copies, waits for them, and re-layouts, relayed(): return jnp.swapaxes(attended, 0, 1)  1.55 us

profile of v8, /device:TPU:17, one launch (start us, length us, event | category | flops | bytes accessed | tf_op | source)
XLA Modules:
  0.0 48.1 jit_solution(6912215000238335396)
XLA Ops:
  0.0 0.0 copy-start.1
  0.0 0.0 copy-start.2
  0.0 0.0 copy-start
  0.0 0.7 %copy-done.1 = s32[2048]{0:T(1024)S(1)} copy-done((s32[2048]{0:T(1024)S(1)}, s32[2048]{0:T(1024)}, u32[]{:S(2)}) %copy-start.1) | copy-done | bytes 8216
  0.7 0.1 dynamic_slice.3
  0.8 0.2 convert_reduce_fusion
  1.0 0.0 copy-done.2
  1.0 0.1 copy.14.start_ref
  1.1 0.0 copy-done
  1.1 1.0 %copy.20 = bf16[64,8,256]{2,0,1:T(8,128)(2,1)S(1)} copy(bf16[64,8,256]{2,1,0:T(8,128)(2,1)} %param.6) | data formatting | bytes 524288 | tf_op args[1]
  2.1 1.8 %copy.19 = bf16[64,8,1024]{2,0,1:T(8,128)(2,1)S(1)} copy(bf16[64,8,1024]{2,1,0:T(8,128)(2,1)} %param.5) | data formatting | bytes 2097152 | tf_op args[0]
  3.9 42.6 %shard_map.55 = bf16[8,64,1024]{2,1,0:T(8,128)(2,1)S(1)} custom-call(bf16[8,64,1024]{2,1,0:T(8,128)(2,1)S(1)} %bitcast.14, bf16[8,64,256]{2,1,0:T(8,128)(2,1)S(1)} %bitcast.15, s32[64,1]{1,0:T(8,128)S(1)} %copy.14.start_ref, bf16[4,16,256]{2,1,0:T(8,128)(2,1)S(1)} %bitcast.16, s32[8,128]{1,0:T(8,128)S(1)} %pad.4.table_ref), custom_call_target="tpu_custom_call" | custom-call | flops 2818572288 | bytes 2097152 | tf_op jit(solution)/shard_map/pallas_call | solution.py:516
  46.6 1.5 %copy.15 = bf16[64,8,1024]{2,1,0:T(8,128)(2,1)} copy(bf16[64,8,1024]{2,0,1:T(8,128)(2,1)S(1)} %bitcast.13) | data formatting | bytes 2097152 | tf_op jit(solution)/shard_map/transpose | solution.py:549
  (2 shorter events, 0.0 us)
Async XLA Ops:
  0.0 0.7 %copy-start.1 = (s32[2048]{0:T(1024)S(1)}, s32[2048]{0:T(1024)}, u32[]{:S(2)}) copy-start(s32[2048]{0:T(1024)} %param.7) | copy-start | bytes 24580
  0.0 1.0 %copy-start.2 = (s32[4,8]{1,0:T(4,128)S(1)}, s32[4,8]{1,0:T(4,128)}, u32[]{:S(2)}) copy-start(s32[4,8]{1,0:T(4,128)} %param.9) | copy-start | bytes 388
  0.0 1.1 %copy-start = (bf16[1,16,4,256]{3,2,1,0:T(4,128)(2,1)S(1)}, bf16[1,16,4,256]{3,2,1,0:T(4,128)(2,1)}, u32[]{:S(2)}) copy-start(bf16[1,16,4,256]{3,2,1,0:T(4,128)(2,1)} %param.8) | copy-start | bytes 98308

commit v9 on v8

--- a/solution.py
+++ b/solution.py
@@ -218,7 +218,8 @@
     started = []
 
     def start(kind, k, j):
-        started.append((kind, k))
+        if (kind, k) not in started:
+            started.append((kind, k))
 
         @pl.when(sends(kind, k))
         def _():
@@ -379,9 +380,8 @@
 
     pool_arrived(3)
 
-    @for_pieces
-    def _(j):
-        corner(2, j)
+    corner(2, 0)
+    corner(2, 1)
 
     table_in.wait_recv()
     pages = PLANES * 4
@@ -407,11 +407,12 @@
             pool_message(SIB_DOWN + d - 1, layer_at(z + d, 1 - c), sib).wait_recv()
     pool_message(SIB_OWN, layer_at(z, 1 - c), sib).wait_recv()
 
-    @for_pieces
-    def _(j):
+    def from_sibling(j):
         for k in range(3):
             for kind in (KSZ, KSX, KSY, KSD):
                 arrived(kind, k, j)
+
+    from_sibling(0)
 
     factor = HEAD_DIM ** (-0.5) * 1.4426950408889634
     group = query_ref.shape[2] // HEAD_DIM
@@ -456,6 +457,14 @@
     score(0, 0)
 
     def two_heads(i, carry):
+        @pl.when(i < PIECES - 2)
+        def _():
+            corner(2, i + 2)
+
+        @pl.when(i < PIECES - 1)
+        def _():
+            from_sibling(i + 1)
+
         h = 2 * i
         score(h + 1, 1)
         soften(h, 0)

time: 48.4 us -> 46.8 us (0.967)
  Pallas kernels: 42.6 us -> 40.6 us
    pallas_call x1, Pallas kernels: 42.6 us -> 40.6 us  [relayed(): pl.pallas_call(functools.partial(relay_kernel, page_table.shape[1]), out_...]
where the time goes in v9:
time: 46.8 us; the launch traced here: 46.1 us
  Pallas kernels  40.6 us (87%)
  local copies, waits for them, and re-layouts  5.23 us (11%)
    pallas_call x1, Pallas kernels, relayed(): pl.pallas_call(functools.partial(relay_kernel, page_table.shape[1]), out_...  40.6 us
    unnamed x9, local copies, waits for them, and re-layouts  3.51 us
    transpose x1, local copies, waits for them, and re-layouts, relayed(): return jnp.swapaxes(attended, 0, 1)  1.55 us

profile of v9, /device:TPU:17, one launch (start us, length us, event | category | flops | bytes accessed | tf_op | source)
XLA Modules:
  0.0 46.1 jit_solution(10102816452439812907)
XLA Ops:
  0.0 0.0 copy-start.1
  0.0 0.0 copy-start.2
  0.0 0.0 copy-start
  0.0 0.7 %copy-done.1 = s32[2048]{0:T(1024)S(1)} copy-done((s32[2048]{0:T(1024)S(1)}, s32[2048]{0:T(1024)}, u32[]{:S(2)}) %copy-start.1) | copy-done | bytes 8216
  0.7 0.1 dynamic_slice.3
  0.8 0.2 convert_reduce_fusion
  1.0 0.0 copy-done.2
  1.0 0.1 copy.14.start_ref
  1.1 0.0 copy-done
  1.1 1.0 %copy.20 = bf16[64,8,256]{2,0,1:T(8,128)(2,1)S(1)} copy(bf16[64,8,256]{2,1,0:T(8,128)(2,1)} %param.6) | data formatting | bytes 524288 | tf_op args[1]
  2.1 1.8 %copy.19 = bf16[64,8,1024]{2,0,1:T(8,128)(2,1)S(1)} copy(bf16[64,8,1024]{2,1,0:T(8,128)(2,1)} %param.5) | data formatting | bytes 2097152 | tf_op args[0]
  3.9 40.6 %shard_map.55 = bf16[8,64,1024]{2,1,0:T(8,128)(2,1)S(1)} custom-call(bf16[8,64,1024]{2,1,0:T(8,128)(2,1)S(1)} %bitcast.14, bf16[8,64,256]{2,1,0:T(8,128)(2,1)S(1)} %bitcast.15, s32[64,1]{1,0:T(8,128)S(1)} %copy.14.start_ref, bf16[4,16,256]{2,1,0:T(8,128)(2,1)S(1)} %bitcast.16, s32[8,128]{1,0:T(8,128)S(1)} %pad.4.table_ref), custom_call_target="tpu_custom_call" | custom-call | flops 2818572288 | bytes 2097152 | tf_op jit(solution)/shard_map/pallas_call | solution.py:525
  44.6 1.5 %copy.15 = bf16[64,8,1024]{2,1,0:T(8,128)(2,1)} copy(bf16[64,8,1024]{2,0,1:T(8,128)(2,1)S(1)} %bitcast.13) | data formatting | bytes 2097152 | tf_op jit(solution)/shard_map/transpose | solution.py:558
  (2 shorter events, 0.0 us)
Async XLA Ops:
  0.0 0.7 %copy-start.1 = (s32[2048]{0:T(1024)S(1)}, s32[2048]{0:T(1024)}, u32[]{:S(2)}) copy-start(s32[2048]{0:T(1024)} %param.7) | copy-start | bytes 24580
  0.0 1.0 %copy-start.2 = (s32[4,8]{1,0:T(4,128)S(1)}, s32[4,8]{1,0:T(4,128)}, u32[]{:S(2)}) copy-start(s32[4,8]{1,0:T(4,128)} %param.9) | copy-start | bytes 388
  0.0 1.1 %copy-start = (bf16[1,16,4,256]{3,2,1,0:T(4,128)(2,1)S(1)}, bf16[1,16,4,256]{3,2,1,0:T(4,128)(2,1)}, u32[]{:S(2)}) copy-start(bf16[1,16,4,256]{3,2,1,0:T(4,128)(2,1)} %param.8) | copy-start | bytes 98308
